TPU v7x, 512 devices: a whole 4x4x16 slice. The times are simulated.
512 devices in a mesh: shard: 128 (over x, z, core), head: 4 (over y).
Axes of the slice: x: 4, y: 4, z: 16, core: 2. Of those that a mesh axis runs over, the one named last changes fastest.
Arguments:
- features: bfloat16 [32768, 1024], P('shard'), may hold values from -6 to 6
- owners: int32 [32768, 1], P('shard'), may hold values from 0 to 127; in each aligned block of 256 rows (0 to 255, 256 to 511, ...) at most 3 rows name the same one
- query_local: int32 [32768], P('shard'), may hold values from 0 to 15
- grades: int32 [32768], P('shard'), may hold values from 0 to 4
- query_weight: float32 [2048], P('shard'), may hold values from 0.3 to 36
- norm_gain: float32 [1024], replicated, may hold values from 0.25 to 1.75
- qkv_weight: bfloat16 [1024, 3, 1024], P(None, None, 'head'), may hold values from -1 to 1
- out_weight: bfloat16 [1024, 1024], P('head'), may hold values from -0.1875 to 0.1875
- score_weight: float32 [1024], P('head'), may hold values from -0.1875 to 0.1875
Outputs:
- encoded: bfloat16 [32768, 1024], P('shard', 'head')
- score_vals: float32 [32768], P('shard')
- score_grads: float32 [32768], P('shard')
- loss: float32 [], replicated
Inputs may be any that keep to these rules, and one draw needn't show every extreme that they name: `owners`: in the rows of one crawl shard no owner is named more than 3 times, a bound that some block reaches.
All inputs are finite; a program needn't handle non-finite values.
Results may differ from a plain program's by a relative error of at most 0.03.
Values may be sent and summed in bfloat16 or wider, within the bound.
A program may use at most 64 MiB of HBM per device.

v0:
```python
import math

import jax
import jax.numpy as jnp
from jax import lax
from jax.sharding import PartitionSpec as P

HEAD_DIM = 64


eps_norm = 1e-06


def block_rows(whole_rows):
    number_blocks = max(1, whole_rows // 512)
    while whole_rows % number_blocks != 0:
        number_blocks = number_blocks - 1
    return whole_rows // number_blocks


def body(
    features,
    owners,
    query_local,
    grades,
    query_weight,
    norm_gain,
    qkv_weight,
    out_weight,
    score_weight,
):
    shards = lax.axis_size("shard")
    head_count = lax.axis_size("head")
    doc_rows = features.shape[0]
    slot_rows = 3 * doc_rows // 2
    capacity = slot_rows // shards
    local_width = out_weight.shape[0]
    model_width = out_weight.shape[1]
    local_heads = local_width // HEAD_DIM
    head_index = lax.axis_index("head")
    query_count = query_weight.shape[0]
    owner_ids = owners[:, 0]
    onehot = (owner_ids[:, None] == jnp.arange(shards, dtype=jnp.int32)[None, :]).astype(jnp.int32)
    bucket_rank = jnp.sum((jnp.cumsum(onehot, axis=0) - onehot) * onehot, axis=1)
    slot_index = owner_ids * capacity + bucket_rank
    meta_rows = jnp.stack([query_local + 1, grades], axis=1).astype(jnp.bfloat16)
    send_meta = jnp.zeros((slot_rows, 2), jnp.bfloat16).at[slot_index].set(meta_rows)
    send_rows = jnp.zeros((slot_rows, model_width), jnp.bfloat16).at[slot_index].set(features)
    rows_full, recv_meta = (
        lax.all_to_all(send_rows, "shard", split_axis=0, concat_axis=0, tiled=True),
        lax.all_to_all(send_meta, "shard", split_axis=0, concat_axis=0, tiled=True),
    )
    query_ids = recv_meta[:, 0].astype(jnp.int32) - 1
    grade_vals = recv_meta[:, 1].astype(jnp.int32)
    row_weight = jnp.sum(
        (query_ids[:, None] == jnp.arange(query_count, dtype=jnp.int32)[None, :]).astype(
            jnp.float32
        )
        * query_weight[None, :],
        axis=1,
    )
    rows_f = rows_full.astype(jnp.float32)
    normed = (
        rows_f * lax.rsqrt(jnp.mean(rows_f * rows_f, axis=1, keepdims=True) + eps_norm) * norm_gain
    ).astype(jnp.bfloat16)
    projected = jnp.dot(
        normed, qkv_weight.reshape(model_width, 3 * local_width), preferred_element_type=jnp.float32
    ).astype(jnp.bfloat16)
    projected = projected.reshape(slot_rows, 3, local_heads, HEAD_DIM)
    queries = projected[:, 0]
    key_rows = projected[:, 1]
    value_rows = projected[:, 2]
    rows_per = block_rows(slot_rows)
    block_count = slot_rows // rows_per
    slot_pos = jnp.arange(slot_rows, dtype=jnp.int32)
    valid = query_ids >= 0
    block_starts = jnp.arange(block_count, dtype=jnp.int32) * rows_per

    def block_mask(block_ids, start):
        block_pos = start + jnp.arange(rows_per, dtype=jnp.int32)
        return (block_ids[:, None] == query_ids[None, :]) & (block_ids >= 0)[:, None] | (
            block_pos[:, None] == slot_pos[None, :]
        )

    def attend(items):
        block_queries, block_ids, start = items
        scores = jnp.einsum(
            "shd,thd->hst", block_queries, key_rows, preferred_element_type=jnp.float32
        ) / math.sqrt(HEAD_DIM)
        same = block_mask(block_ids, start)
        scores = jnp.where(same[None], scores, -jnp.inf)
        peak = jnp.max(scores, axis=2, keepdims=True)
        expo = jnp.exp(scores - peak)
        probs = (expo / jnp.sum(expo, axis=2, keepdims=True)).astype(jnp.bfloat16)
        return jnp.einsum(
            "hst,thd->shd", probs, value_rows, preferred_element_type=jnp.float32
        ).astype(jnp.bfloat16)

    context = lax.map(
        attend,
        (
            queries.reshape(block_count, rows_per, local_heads, HEAD_DIM),
            query_ids.reshape(block_count, rows_per),
            block_starts,
        ),
    )
    context = context.reshape(slot_rows, local_width)
    partial_out = jnp.dot(context, out_weight, preferred_element_type=jnp.float32)
    attended = lax.psum_scatter(
        partial_out.astype(jnp.bfloat16), "head", scatter_dimension=1, tiled=True
    ).astype(jnp.float32)
    own_full = lax.dynamic_slice_in_dim(rows_full, head_index * local_width, local_width, 1)
    mixed = own_full.astype(jnp.float32) + attended
    encoded_slots = mixed.astype(jnp.bfloat16)
    square_sum, weighted_sum = lax.psum(
        (jnp.sum(mixed * mixed, axis=1), jnp.dot(mixed, score_weight)), "head"
    )
    score_row = weighted_sum * lax.rsqrt(square_sum / (local_width * head_count) + eps_norm)

    def pair_block(items):
        block_scores, block_grades, block_ids, block_weight, start = items
        same = block_mask(block_ids, start)
        better = (
            same
            & (block_ids >= 0)[:, None]
            & valid[None, :]
            & (block_grades[:, None] > grade_vals[None, :])
        ).astype(jnp.float32)
        weighted = better * block_weight[:, None]
        spread = score_row[None, :] - block_scores[:, None]
        pulled = weighted * jax.nn.sigmoid(spread)
        return (
            jnp.sum(weighted * jax.nn.softplus(spread)),
            jnp.sum(better),
            jnp.sum(pulled, axis=1),
            jnp.sum(pulled, axis=0),
        )

    block_sums, block_counts, row_pulls, column_pulls = lax.map(
        pair_block,
        (
            score_row.reshape(block_count, rows_per),
            grade_vals.reshape(block_count, rows_per),
            query_ids.reshape(block_count, rows_per),
            row_weight.reshape(block_count, rows_per),
            block_starts,
        ),
    )
    pair_sum = jnp.sum(block_sums)
    pair_count = jnp.sum(block_counts)
    pull = jnp.sum(column_pulls, axis=0) - row_pulls.reshape(slot_rows)
    total_sum, total_count = lax.psum((pair_sum, pair_count), "shard")
    pair_total = jnp.maximum(total_count, jnp.float32(1.0))
    loss = total_sum / pair_total
    grad_slots = pull / pair_total
    back_enc = lax.all_to_all(encoded_slots, "shard", split_axis=0, concat_axis=0, tiled=True)
    back_pair = lax.all_to_all(
        jnp.stack([score_row, grad_slots], axis=1), "shard", split_axis=0, concat_axis=0, tiled=True
    )
    encoded = back_enc[slot_index]
    picked = back_pair[slot_index]
    return (encoded, picked[:, 0], picked[:, 1], loss)


def solution(mesh):
    placed = (
        P("shard", None),
        P("shard", None),
        P("shard"),
        P("shard"),
        P("shard"),
        P(),
        P(None, None, "head"),
        P("head", None),
        P("head"),
    )
    return jax.shard_map(
        body,
        mesh=mesh,
        in_specs=placed,
        out_specs=(P("shard", "head"), P("shard"), P("shard"), P()),
        check_vma=False,
    )
```

profile of v0, /device:TPU:1, one launch (start us, length us, event | category | flops | bytes accessed | tf_op | source)
XLA Modules:
  0.0 468.7 jit_solution(1439142511192248365)
XLA Ops:
  9.9 0.9 fusion.28
  11.4 1.2 scatter_custom_fusion.1
  13.7 20.4 %all-to-all-start.1 = ((bf16[128,3,2]{1,2,0:T(2,128)(2,1)}), bf16[128,3,2]{1,2,0:T(2,128)(2,1)S(1)}, u32[]{:S(2)}, u32[]{:S(2)}) async-start(bf16[128,3,2]{1,2,0:T(2,128)(2,1)} %copy.79), calls=%async_computation.1 | async-start | bytes 131072 | tf_op jit(solution)/shard_map/all_to_all | solution.py:51
  34.1 2.4 scatter_custom_fusion
  36.5 1.3 all_to_all.30
  37.8 11.2 %all-to-all-done.1 = bf16[128,3,2]{1,2,0:T(2,128)(2,1)S(1)} async-done(((bf16[128,3,2]{1,2,0:T(2,128)(2,1)}), bf16[128,3,2]{1,2,0:T(2,128)(2,1)S(1)}, u32[]{:S(2)}, u32[]{:S(2)}) %all-to-all-start.1) | async-done | bytes 1568 | tf_op jit(solution)/shard_map/all_to_all | solution.py:51
  49.0 6.6 %all-to-all-start = ((bf16[128,3,1024]{2,1,0:T(4,128)(2,1)}), bf16[128,3,1024]{2,1,0:T(4,128)(2,1)S(1)}, u32[]{:S(2)}, u32[]{:S(2)}) async-start(bf16[128,3,1024]{2,1,0:T(4,128)(2,1)} %all_to_all.30), calls=%async_computation | async-start | bytes 2097152 | tf_op jit(solution)/shard_map/all_to_all | solution.py:50
  55.9 1.8 copy.75
  58.7 51.4 %all-to-all-done = bf16[128,3,1024]{2,1,0:T(4,128)(2,1)S(1)} async-done(((bf16[128,3,1024]{2,1,0:T(4,128)(2,1)}), bf16[128,3,1024]{2,1,0:T(4,128)(2,1)S(1)}, u32[]{:S(2)}, u32[]{:S(2)}) %all-to-all-start) | async-done | bytes 786464 | tf_op jit(solution)/shard_map/all_to_all | solution.py:50
  112.1 2.2 convolution_convert_fusion.1
  114.6 0.9 fusion.45
  115.5 1.2 fusion.9
  116.8 1.3 convolution_convert_fusion
  118.9 21.8 %reduce-scatter.2.cloned.1.call-done = bf16[384,256]{1,0:T(8,128)(2,1)} async-done(((bf16[384,1024]{1,0:T(8,128)(2,1)}), bf16[384,256]{1,0:T(8,128)(2,1)}) %reduce-scatter.2.cloned.1.call-update) | async-done | bytes 196624 | tf_op jit(solution)/shard_map/reduce_scatter | solution.py:109
  140.7 1.1 multiply_reduce_fusion
  141.8 1.1 convolution_reduce_fusion
  142.9 6.0 %all-reduce.1 = (f32[384]{0:T(512)S(1)}, f32[384]{0:T(512)S(1)}) all-reduce(f32[384]{0:T(512)S(1)} %convolution_reduce_fusion, f32[384]{0:T(512)S(1)} %get-tuple-element.68), channel_id=1, replica_groups=mesh['shard'=128,'head'=4] {'head'}, use_global_device_ids=true, to_apply=%region_9.10 | all-reduce | flops 768 | bytes 6144 | tf_op jit(solution)/shard_map/psum | solution.py:115
  149.1 1.5 fusion.10
  150.6 251.9 %all-reduce = (f32[]{:T(128)}, f32[]{:T(128)}) all-reduce(f32[]{:T(128)} %get-tuple-element.61, f32[]{:T(128)} %get-tuple-element.44), channel_id=1, replica_groups=mesh['shard'=128,'head'=4] {'shard'}, use_global_device_ids=true, to_apply=%region_16.17 | all-reduce | flops 2 | bytes 16 | tf_op jit(solution)/shard_map/psum | solution.py:152
  404.2 7.5 %all-to-all-start.3 = ((f32[128,3,2]{1,2,0:T(2,128)}), f32[128,3,2]{1,2,0:T(2,128)S(1)}, u32[]{:S(2)}, u32[]{:S(2)}) async-start(f32[128,3,2]{1,2,0:T(2,128)} %copy.82), calls=%async_computation.4 | async-start | bytes 262144 | tf_op jit(solution)/shard_map/all_to_all | solution.py:157
  412.5 16.7 %all-to-all-done.3 = f32[128,3,2]{1,2,0:T(2,128)S(1)} async-done(((f32[128,3,2]{1,2,0:T(2,128)}), f32[128,3,2]{1,2,0:T(2,128)S(1)}, u32[]{:S(2)}, u32[]{:S(2)}) %all-to-all-start.3) | async-done | bytes 3104 | tf_op jit(solution)/shard_map/all_to_all | solution.py:157
  429.2 6.9 %all-to-all-start.2 = ((bf16[128,3,256]{2,1,0:T(4,128)(2,1)}), bf16[128,3,256]{2,1,0:T(4,128)(2,1)S(1)}, u32[]{:S(2)}, u32[]{:S(2)}) async-start(bf16[128,3,256]{2,1,0:T(4,128)(2,1)} %all_to_all.36), calls=%async_computation.3 | async-start | bytes 524288 | tf_op jit(solution)/shard_map/all_to_all | solution.py:156
  438.7 20.0 %all-to-all-done.2 = bf16[128,3,256]{2,1,0:T(4,128)(2,1)S(1)} async-done(((bf16[128,3,256]{2,1,0:T(4,128)(2,1)}), bf16[128,3,256]{2,1,0:T(4,128)(2,1)S(1)}, u32[]{:S(2)}, u32[]{:S(2)}) %all-to-all-start.2) | async-done | bytes 196640 | tf_op jit(solution)/shard_map/all_to_all | solution.py:156
  458.9 1.8 gather_fusion
  (71 shorter events, 12.8 us)
Async XLA Ops:
  7.2 109.6 %copy-start = (bf16[256,1024]{1,0:T(8,128)(2,1)S(1)}, bf16[256,1024]{1,0:T(8,128)(2,1)}, u32[]{:S(2)}) copy-start(bf16[256,1024]{1,0:T(8,128)(2,1)} %param.16) | copy-start | bytes 1572868
  11.4 26.4 %copy-start.5 = (s32[256,1]{0,1:T(1,128)}, s32[256,1]{0,1:T(1,128)S(1)}, u32[]{:S(2)}) copy-start(s32[256,1]{0,1:T(1,128)S(1)} %compare_select_fusion.1) | copy-start | bytes 3076
  13.7 35.4 %all-to-all-start.1 = ((bf16[128,3,2]{1,2,0:T(2,128)(2,1)}), bf16[128,3,2]{1,2,0:T(2,128)(2,1)S(1)}, u32[]{:S(2)}, u32[]{:S(2)}) async-start(bf16[128,3,2]{1,2,0:T(2,128)(2,1)} %copy.79), calls=%async_computation.1 | async-start | bytes 131072 | tf_op jit(solution)/shard_map/all_to_all | solution.py:51
  36.5 19.4 %copy-start.1 = (bf16[1024,3,256]{2,0,1:T(8,128)(2,1)S(1)}, bf16[1024,3,256]{2,0,1:T(8,128)(2,1)}, u32[]{:S(2)}) copy-start(bf16[1024,3,256]{2,0,1:T(8,128)(2,1)} %param.15) | copy-start | bytes 4718596
  49.0 61.0 %all-to-all-start = ((bf16[128,3,1024]{2,1,0:T(4,128)(2,1)}), bf16[128,3,1024]{2,1,0:T(4,128)(2,1)S(1)}, u32[]{:S(2)}, u32[]{:S(2)}) async-start(bf16[128,3,1024]{2,1,0:T(4,128)(2,1)} %all_to_all.30), calls=%async_computation | async-start | bytes 2097152 | tf_op jit(solution)/shard_map/all_to_all | solution.py:50
  55.6 85.0 %reduce-scatter.2.cloned.1.call-start = ((), (), s32[]{:S(2)}) async-start(), calls=%async_computation.5 | async-start | bytes 983040 | tf_op jit(solution)/shard_map/reduce_scatter | solution.py:109
  57.6 53.1 %copy-start.4 = (f32[1024]{0:T(1024)S(1)}, f32[1024]{0:T(1024)}, u32[]{:S(2)}) copy-start(f32[1024]{0:T(1024)} %param.14) | copy-start | bytes 12292
  57.9 52.2 %copy-start.7 = (pred[384]{0:T(512)(128)(4,1)}, pred[384]{0:T(512)(128)(4,1)S(1)}, u32[]{:S(2)}) copy-start(pred[384]{0:T(512)(128)(4,1)S(1)} %compare_reduce_fusion) | copy-start | bytes 1156
  58.5 51.6 %copy-start.2 = (s32[384]{0:T(512)}, s32[384]{0:T(512)S(1)}, u32[]{:S(2)}) copy-start(s32[384]{0:T(512)S(1)} %get-tuple-element.63) | copy-start | bytes 4612
  116.7 1.4 copy-start.3
  116.7 1.4 copy-start.11
  118.0 23.7 %copy-start.10 = (f32[256]{0:T(256)S(1)}, f32[256]{0:T(256)}, u32[]{:S(2)}) copy-start(f32[256]{0:T(256)} %param.17) | copy-start | bytes 3076
  118.1 31.1 %copy-start.8 = (pred[384]{0:T(512)(128)(4,1)S(1)}, pred[384]{0:T(512)(128)(4,1)}, u32[]{:S(2)}) copy-start(pred[384]{0:T(512)(128)(4,1)} %copy-done.7) | copy-start | bytes 1156
  118.1 31.1 %copy-start.9 = (s32[384]{0:T(512)S(1)}, s32[384]{0:T(512)}, u32[]{:S(2)}) copy-start(s32[384]{0:T(512)} %get-tuple-element.62) | copy-start | bytes 4612
  141.8 294.4 %copy-start.6 = (s32[256,1]{0,1:T(1,128)S(1)}, s32[256,1]{0,1:T(1,128)}, u32[]{:S(2)}) copy-start(s32[256,1]{0,1:T(1,128)} %copy-done.5) | copy-start | bytes 3076
  404.2 25.0 %all-to-all-start.3 = ((f32[128,3,2]{1,2,0:T(2,128)}), f32[128,3,2]{1,2,0:T(2,128)S(1)}, u32[]{:S(2)}, u32[]{:S(2)}) async-start(f32[128,3,2]{1,2,0:T(2,128)} %copy.82), calls=%async_computation.4 | async-start | bytes 262144 | tf_op jit(solution)/shard_map/all_to_all | solution.py:157
  429.2 29.5 %all-to-all-start.2 = ((bf16[128,3,256]{2,1,0:T(4,128)(2,1)}), bf16[128,3,256]{2,1,0:T(4,128)(2,1)S(1)}, u32[]{:S(2)}, u32[]{:S(2)}) async-start(bf16[128,3,256]{2,1,0:T(4,128)(2,1)} %all_to_all.36), calls=%async_computation.3 | async-start | bytes 524288 | tf_op jit(solution)/shard_map/all_to_all | solution.py:156
Sparse Core Ops, SparseCore 0:
  118.2 22.4 reduce-scatter.1
where the time goes:
time: 470 us; the launch traced here: 469 us
  blocking collectives  258 us (55%)
  waiting for transfers between devices  121 us (26%)
  starting transfers between devices  41.6 us (9%)
  between operations  16.8 us (4%)
  local copies, waits for them, and re-layouts  16.5 us (4%)
  other arithmetic  7.98 us (2%)
  matrix products  6.75 us (1%)
    psum x1, blocking collectives, body(): total_sum, total_count = lax.psum((pair_sum, pair_count), 'shard')  252 us
    all_to_all x1, waiting for transfers between devices, body(): lax.all_to_all(send_rows, 'shard', split_axis=0, concat_axis=0, tiled=True)  51.4 us
    reduce_scatter x1, waiting for transfers between devices, body(): lax.psum_scatter(partial_out.astype(jnp.bfloat16), 'head', scatter_dimens...  21.8 us
    all_to_all x1, starting transfers between devices, body(): lax.all_to_all(send_meta, 'shard', split_axis=0, concat_axis=0, tiled=True)  20.4 us
    all_to_all x1, waiting for transfers between devices, body(): lax.all_to_all(encoded_slots, 'shard', split_axis=0, concat_axis=0, tiled...  20 us
    all_to_all x1, waiting for transfers between devices, body(): lax.all_to_all(jnp.stack([score_row, grad_slots], axis=1), 'shard', split...  16.7 us
    all_to_all x1, waiting for transfers between devices, body(): lax.all_to_all(send_meta, 'shard', split_axis=0, concat_axis=0, tiled=True)  11.2 us
  transfers between devices with their start and end apart: 5, of which 5 were waited for; matrix products, arithmetic and copies ran while one was open for 1% of the time, Pallas kernels for 0%

commit v1 on v0

--- a/solution.py
+++ b/solution.py
@@ -44,14 +44,15 @@
     bucket_rank = jnp.sum((jnp.cumsum(onehot, axis=0) - onehot) * onehot, axis=1)
     slot_index = owner_ids * capacity + bucket_rank
     meta_rows = jnp.stack([query_local + 1, grades], axis=1).astype(jnp.bfloat16)
-    send_meta = jnp.zeros((slot_rows, 2), jnp.bfloat16).at[slot_index].set(meta_rows)
-    send_rows = jnp.zeros((slot_rows, model_width), jnp.bfloat16).at[slot_index].set(features)
-    rows_full, recv_meta = (
-        lax.all_to_all(send_rows, "shard", split_axis=0, concat_axis=0, tiled=True),
-        lax.all_to_all(send_meta, "shard", split_axis=0, concat_axis=0, tiled=True),
+    own_cols = lax.dynamic_slice_in_dim(features, head_index * local_width, local_width, 1)
+    send = jnp.zeros((slot_rows, local_width + 2), jnp.bfloat16).at[slot_index].set(
+        jnp.concatenate([own_cols, meta_rows], axis=1)
     )
-    query_ids = recv_meta[:, 0].astype(jnp.int32) - 1
-    grade_vals = recv_meta[:, 1].astype(jnp.int32)
+    recv = lax.all_to_all(send, "shard", split_axis=0, concat_axis=0, tiled=True)
+    own_full = recv[:, :local_width]
+    rows_full = lax.all_gather(own_full, "head", axis=1, tiled=True)
+    query_ids = recv[:, local_width].astype(jnp.int32) - 1
+    grade_vals = recv[:, local_width + 1].astype(jnp.int32)
     row_weight = jnp.sum(
         (query_ids[:, None] == jnp.arange(query_count, dtype=jnp.int32)[None, :]).astype(
             jnp.float32
@@ -109,7 +110,6 @@
     attended = lax.psum_scatter(
         partial_out.astype(jnp.bfloat16), "head", scatter_dimension=1, tiled=True
     ).astype(jnp.float32)
-    own_full = lax.dynamic_slice_in_dim(rows_full, head_index * local_width, local_width, 1)
     mixed = own_full.astype(jnp.float32) + attended
     encoded_slots = mixed.astype(jnp.bfloat16)
     square_sum, weighted_sum = lax.psum(
@@ -149,17 +149,33 @@
     pair_sum = jnp.sum(block_sums)
     pair_count = jnp.sum(block_counts)
     pull = jnp.sum(column_pulls, axis=0) - row_pulls.reshape(slot_rows)
-    total_sum, total_count = lax.psum((pair_sum, pair_count), "shard")
-    pair_total = jnp.maximum(total_count, jnp.float32(1.0))
-    loss = total_sum / pair_total
-    grad_slots = pull / pair_total
-    back_enc = lax.all_to_all(encoded_slots, "shard", split_axis=0, concat_axis=0, tiled=True)
-    back_pair = lax.all_to_all(
-        jnp.stack([score_row, grad_slots], axis=1), "shard", split_axis=0, concat_axis=0, tiled=True
+    sums = jnp.concatenate(
+        [jnp.broadcast_to(v[None], (slot_rows, 1)) for v in (pair_sum, pair_count)], axis=1
     )
-    encoded = back_enc[slot_index]
-    picked = back_pair[slot_index]
-    return (encoded, picked[:, 0], picked[:, 1], loss)
+    words = jnp.concatenate([score_row[:, None], pull[:, None], sums], axis=1)
+    high = lax.reduce_precision(words, 8, 7)
+    middle = lax.reduce_precision(words - high, 8, 7)
+    low = words - high - middle
+    back = lax.all_to_all(
+        jnp.concatenate(
+            [encoded_slots]
+            + [piece.astype(jnp.bfloat16) for piece in (high, middle, low)],
+            axis=1,
+        ),
+        "shard",
+        split_axis=0,
+        concat_axis=0,
+        tiled=True,
+    )
+    tail = back[:, local_width:].astype(jnp.float32)
+    tail = tail[:, 0:4] + tail[:, 4:8] + tail[:, 8:12]
+    totals = jnp.sum(tail.reshape(shards, capacity, 4)[:, 0, 2:4], axis=0)
+    pair_total = jnp.maximum(totals[1], jnp.float32(1.0))
+    loss = totals[0] / pair_total
+    picked = back[slot_index]
+    encoded = picked[:, :local_width]
+    words_back = tail[slot_index]
+    return (encoded, words_back[:, 0], words_back[:, 1] / pair_total, loss)
 
 
 def solution(mesh):

time: 470 us -> 180 us (0.38)
  blocking collectives: 258 us -> 17.5 us
  waiting for transfers between devices: 121 us -> 77.5 us
    psum x1 -> x0, blocking collectives: 252 us -> none  [body(): total_sum, total_count = lax.psum((pair_sum, pair_count), 'shard')]
    all_to_all x4 -> x2, waiting for transfers between devices: 99.4 us -> 53.9 us  [the longest x1 27.8 us: body(): lax.all_to_all(jnp.concatenate([encoded_slots] + [piece.astype(jnp.bfloat...]
    all_gather x0 -> x1, blocking collectives: none -> 11.5 us  [body(): rows_full = lax.all_gather(own_full, 'head', axis=1, tiled=True)]
    all_to_all x4 -> x2, starting transfers between devices: 41.4 us -> 40.3 us  [the longest x1 20.4 us: body(): lax.all_to_all(send, 'shard', split_axis=0, concat_axis=0, tiled=True)]
  transfers between devices with their start and end apart: 5 -> 3, of which waited for: 5 -> 3; matrix products, arithmetic and copies ran while one was open for 1% -> 1% of each run, Pallas kernels for 0% -> 0%
where the time goes in v1:
time: 180 us; the launch traced here: 179 us
  waiting for transfers between devices  77.5 us (43%)
  starting transfers between devices  40.3 us (22%)
  blocking collectives  17.5 us (10%)
  between operations  16.7 us (9%)
  local copies, waits for them, and re-layouts  11.8 us (7%)
  other arithmetic  9.74 us (5%)
  matrix products  5.36 us (3%)
    all_to_all x1, waiting for transfers between devices, body(): lax.all_to_all(jnp.concatenate([encoded_slots] + [piece.astype(jnp.bfloat...  27.8 us
    all_to_all x1, waiting for transfers between devices, body(): lax.all_to_all(send, 'shard', split_axis=0, concat_axis=0, tiled=True)  26 us
    reduce_scatter x1, waiting for transfers between devices, body(): lax.psum_scatter(partial_out.astype(jnp.bfloat16), 'head', scatter_dimens...  23.6 us
    all_to_all x1, starting transfers between devices, body(): lax.all_to_all(send, 'shard', split_axis=0, concat_axis=0, tiled=True)  20.4 us
    all_to_all x1, starting transfers between devices, body(): lax.all_to_all(jnp.concatenate([encoded_slots] + [piece.astype(jnp.bfloat...  19.9 us
    all_gather x1, blocking collectives, body(): rows_full = lax.all_gather(own_full, 'head', axis=1, tiled=True)  11.5 us
    psum x1, blocking collectives, body(): lax.psum((jnp.sum(mixed * mixed, axis=1), jnp.dot(mixed, score_weight)),...  6.01 us
  transfers between devices with their start and end apart: 3, of which 3 were waited for; matrix products, arithmetic and copies ran while one was open for 1% of the time, Pallas kernels for 0%

profile of v1, /device:TPU:1, one launch (start us, length us, event | category | flops | bytes accessed | tf_op | source)
XLA Modules:
  0.0 178.9 jit_solution(6079704360987993311)
XLA Ops:
  7.2 0.8 copy.48
  8.3 1.0 fusion.38
  11.6 0.9 constant_dynamic-slice_fusion
  12.5 1.6 scatter_custom_fusion
  14.1 0.9 all_to_all.16
  15.0 20.4 %all-to-all-start = ((bf16[128,3,258]{2,1,0:T(4,128)(2,1)}), bf16[128,3,258]{2,1,0:T(4,128)(2,1)S(1)}, u32[]{:S(2)}, u32[]{:S(2)}) async-start(bf16[128,3,258]{2,1,0:T(4,128)(2,1)} %all_to_all.16), calls=%async_computation | async-start | bytes 786432 | tf_op jit(solution)/shard_map/all_to_all | solution.py:51
  35.5 1.8 copy.52
  37.3 26.0 %all-to-all-done = bf16[128,3,258]{2,1,0:T(4,128)(2,1)S(1)} async-done(((bf16[128,3,258]{2,1,0:T(4,128)(2,1)}), bf16[128,3,258]{2,1,0:T(4,128)(2,1)S(1)}, u32[]{:S(2)}, u32[]{:S(2)}) %all-to-all-start) | async-done | bytes 198176 | tf_op jit(solution)/shard_map/all_to_all | solution.py:51
  64.0 11.5 %all_gather.3 = bf16[384,1024]{1,0:T(8,128)(2,1)S(1)} all-gather(bf16[384,256]{1,0:T(8,128)(2,1)S(1)} %slice.77), channel_id=1, replica_groups=mesh['shard'=128,'head'=4] {'head'}, dimensions={1}, use_global_device_ids=true | all-gather | bytes 983040 | tf_op jit(solution)/shard_map/all_gather | solution.py:53
  75.7 0.8 convolution_convert_fusion.1
  77.1 0.9 fusion.53
  78.0 1.2 fusion.9
  79.2 1.3 convolution_convert_fusion
  80.6 23.6 %reduce-scatter.2.cloned.1.call-done = bf16[384,256]{1,0:T(8,128)(2,1)} async-done(((bf16[384,1024]{1,0:T(8,128)(2,1)}), bf16[384,256]{1,0:T(8,128)(2,1)}) %reduce-scatter.2.cloned.1.call-update) | async-done | bytes 196624 | tf_op jit(solution)/shard_map/reduce_scatter | solution.py:110
  104.2 1.1 fusion.22
  105.3 1.1 convolution_reduce_fusion
  106.4 6.0 %all-reduce = (f32[384]{0:T(512)S(1)}, f32[384]{0:T(512)S(1)}) all-reduce(f32[384]{0:T(512)S(1)} %convolution_reduce_fusion, f32[384]{0:T(512)S(1)} %get-tuple-element.69), channel_id=1, replica_groups=mesh['shard'=128,'head'=4] {'head'}, use_global_device_ids=true, to_apply=%region_8.9 | all-reduce | flops 768 | bytes 6144 | tf_op jit(solution)/shard_map/psum | solution.py:115
  112.4 1.5 fusion.13
  116.2 0.9 all_to_all.19
  117.1 19.9 %all-to-all-start.1 = ((bf16[128,3,268]{2,1,0:T(4,128)(2,1)}), bf16[128,3,268]{2,1,0:T(4,128)(2,1)S(1)}, u32[]{:S(2)}, u32[]{:S(2)}) async-start(bf16[128,3,268]{2,1,0:T(4,128)(2,1)} %all_to_all.19), calls=%async_computation.2 | async-start | bytes 786432 | tf_op jit(solution)/shard_map/all_to_all | solution.py:159
  137.0 27.8 %all-to-all-done.1 = bf16[128,3,268]{2,1,0:T(4,128)(2,1)S(1)} async-done(((bf16[128,3,268]{2,1,0:T(4,128)(2,1)}), bf16[128,3,268]{2,1,0:T(4,128)(2,1)S(1)}, u32[]{:S(2)}, u32[]{:S(2)}) %all-to-all-start.1) | async-done | bytes 205856 | tf_op jit(solution)/shard_map/all_to_all | solution.py:159
  165.4 0.8 gather_fusion.1
  166.1 1.2 gather_fusion
  169.5 0.8 fusion.40
  (57 shorter events, 8.5 us)
Async XLA Ops:
  7.2 72.1 %copy-start = (bf16[256,1024]{1,0:T(8,128)(2,1)S(1)}, bf16[256,1024]{1,0:T(8,128)(2,1)}, u32[]{:S(2)}) copy-start(bf16[256,1024]{1,0:T(8,128)(2,1)} %param.16) | copy-start | bytes 1572868
  8.2 27.3 %copy-start.1 = (bf16[1024,3,256]{2,0,1:T(8,128)(2,1)S(1)}, bf16[1024,3,256]{2,0,1:T(8,128)(2,1)}, u32[]{:S(2)}) copy-start(bf16[1024,3,256]{2,0,1:T(8,128)(2,1)} %param.15) | copy-start | bytes 4718596
  15.0 48.3 %all-to-all-start = ((bf16[128,3,258]{2,1,0:T(4,128)(2,1)}), bf16[128,3,258]{2,1,0:T(4,128)(2,1)S(1)}, u32[]{:S(2)}, u32[]{:S(2)}) async-start(bf16[128,3,258]{2,1,0:T(4,128)(2,1)} %all_to_all.16), calls=%async_computation | async-start | bytes 786432 | tf_op jit(solution)/shard_map/all_to_all | solution.py:51
  35.4 68.8 %reduce-scatter.2.cloned.1.call-start = ((), (), s32[]{:S(2)}) async-start(), calls=%async_computation.3 | async-start | bytes 983040 | tf_op jit(solution)/shard_map/reduce_scatter | solution.py:110
  37.3 38.5 %copy-start.2 = (bf16[1024,3,256]{0,2,1:T(8,128)(2,1)S(1)}, bf16[1024,3,256]{0,2,1:T(8,128)(2,1)}, u32[]{:S(2)}) copy-start(bf16[1024,3,256]{0,2,1:T(8,128)(2,1)} %copy.52) | copy-start | bytes 4718596
  37.3 38.5 %copy-start.4 = (f32[1024]{0:T(1024)S(1)}, f32[1024]{0:T(1024)}, u32[]{:S(2)}) copy-start(f32[1024]{0:T(1024)} %param.14) | copy-start | bytes 12292
  79.2 1.3 copy-start.3
  79.2 26.1 %copy-start.5 = (f32[256]{0:T(256)S(1)}, f32[256]{0:T(256)}, u32[]{:S(2)}) copy-start(f32[256]{0:T(256)} %param.17) | copy-start | bytes 3076
  117.1 47.7 %all-to-all-start.1 = ((bf16[128,3,268]{2,1,0:T(4,128)(2,1)}), bf16[128,3,268]{2,1,0:T(4,128)(2,1)S(1)}, u32[]{:S(2)}, u32[]{:S(2)}) async-start(bf16[128,3,268]{2,1,0:T(4,128)(2,1)} %all_to_all.19), calls=%async_computation.2 | async-start | bytes 786432 | tf_op jit(solution)/shard_map/all_to_all | solution.py:159
Sparse Core Ops, SparseCore 0:
  80.7 23.5 reduce-scatter.1

commit v2 on v0

v2 whole, which is shorter than its diff:
```python
import functools

import jax
import jax.numpy as jnp
from jax import lax
from jax.experimental import pallas as pl
from jax.experimental.pallas import tpu as pltpu
from jax.sharding import PartitionSpec as P

MESH = pl.DeviceIdType.MESH
HEAD_DIM = 64
CAP = 3
ROWS = 8
LANES = 128
eps_norm = 1e-06
F32 = jnp.float32
BF16 = jnp.bfloat16
NT = (((1,), (1,)), ((), ()))
TN = (((0,), (0,)), ((), ()))


def dot(a, b):
    return jnp.dot(a, b, preferred_element_type=F32)


def iota(shape, dim):
    return lax.broadcasted_iota(jnp.int32, shape, dim)


def layer_kernel(
    shards,
    heads,
    feat_ref,
    doc_ref,
    qw_ref,
    gain_ref,
    wqkv_hbm,
    wout_hbm,
    sw_ref,
    enc_ref,
    small_ref,
    wqkv,
    wout,
    send,
    recv,
    wide,
    gathered,
    proj,
    parts,
    landed,
    stats,
    back_send,
    back,
    local_sem,
    send_sem,
    recv_sem,
    y_send,
    y_recv,
):
    me = lax.axis_index("shard")
    head = lax.axis_index("head")
    docs = feat_ref.shape[0]
    width = wout_hbm.shape[0]
    model = wout_hbm.shape[1]
    slots = CAP * shards

    def peer(i):
        return lax.rem(me + i, shards)

    def head_peer(i):
        return lax.rem(head + i, heads)

    barrier = pltpu.get_barrier_semaphore()

    def greet(i, carry):
        pl.semaphore_signal(
            barrier, 1, device_id={"shard": peer(i)}, device_id_type=MESH
        )
        return carry

    lax.fori_loop(1, shards, greet, 0)
    for i in range(1, heads):
        pl.semaphore_signal(
            barrier, 1, device_id={"head": head_peer(i)}, device_id_type=MESH
        )
    load_qkv = pltpu.make_async_copy(wqkv_hbm, wqkv, local_sem.at[0])
    load_out = pltpu.make_async_copy(wout_hbm, wout, local_sem.at[1])
    load_qkv.start()
    load_out.start()

    owner = jnp.bitwise_and(doc_ref[0:1, :] - me, shards - 1)
    query = doc_ref[1:2, :].astype(F32) + 1.0
    grade = doc_ref[2:3, :].astype(F32)
    named = iota((shards, docs), 0) == owner
    named_f = named.astype(F32)
    earlier = (iota((docs, docs), 0) < iota((docs, docs), 1)).astype(F32).astype(BF16)
    before = dot(named_f.astype(BF16), earlier)
    rank_f = jnp.sum(before * named_f, axis=0, keepdims=True)
    rank = rank_f.astype(jnp.int32)
    first = owner * ROWS + 2 * rank
    block_row = iota((shards * ROWS, docs), 0)
    place = [
        (block_row == where).astype(F32).astype(BF16)
        for where in (first, first + 1, owner * ROWS + 2 * CAP)
    ]
    lane = iota((LANES, docs), 0)
    facts = jnp.where(lane == rank, query, 0.0) + jnp.where(
        lane == rank + CAP, grade, 0.0
    )
    left = pl.ds(pl.multiple_of(head * width, LANES), LANES)
    right = pl.ds(pl.multiple_of(head * width + LANES, LANES), LANES)
    block = dot(place[0], feat_ref[:, left]) + dot(place[1], feat_ref[:, right])
    block = block + lax.dot_general(
        place[2], facts.astype(BF16), NT, preferred_element_type=F32
    )
    send[...] = block.reshape(shards, ROWS, LANES).astype(BF16)

    pl.semaphore_wait(barrier, shards - 1 + heads - 1)

    def push(i, carry):
        pltpu.make_async_remote_copy(
            send.at[i],
            recv.at[i],
            send_sem.at[0],
            recv_sem.at[0],
            device_id={"shard": peer(i)},
            device_id_type=MESH,
        ).start()
        return carry

    lax.fori_loop(1, shards, push, 0)
    recv[0] = send[0]
    others = recv.at[pl.ds(1, shards - 1)]
    pltpu.make_async_copy(others, others, recv_sem.at[0]).wait()

    wide[...] = recv[...].astype(F32).reshape(shards * ROWS, LANES)

    def rows_of(j):
        return wide[pl.ds(j, shards, stride=ROWS), :]

    own = gathered.at[head]
    for r in range(CAP):
        for half in range(2):
            own[r * shards : (r + 1) * shards, half * LANES : (half + 1) * LANES] = (
                rows_of(2 * r + half).astype(BF16)
            )
    fact_cols = rows_of(2 * CAP)
    fact_rows = fact_cols.T

    def exchange(source, target, lane_of):
        copies = []
        for i in (2, 1, 3):
            copy = pltpu.make_async_remote_copy(
                source(head_peer(i)),
                target,
                y_send.at[lane_of, i],
                y_recv.at[lane_of, i],
                device_id={"head": head_peer(i)},
                device_id_type=MESH,
            )
            copy.start()
            copies.append(copy)
        return copies

    copies = exchange(lambda t: own, own, 0)
    query_col = jnp.concatenate([fact_cols[:, r : r + 1] for r in range(CAP)], axis=0)
    query_row = jnp.concatenate([fact_rows[r : r + 1, :] for r in range(CAP)], axis=1)
    grade_col = jnp.concatenate(
        [fact_cols[:, CAP + r : CAP + r + 1] for r in range(CAP)], axis=0
    )
    grade_row = jnp.concatenate(
        [fact_rows[CAP + r : CAP + r + 1, :] for r in range(CAP)], axis=1
    )
    diagonal = iota((slots, slots), 0) == iota((slots, slots), 1)
    related = (query_col == query_row) & (query_col > 0.5)
    bias = jnp.where(related | diagonal, 0.0, -jnp.inf)
    load_qkv.wait()
    load_out.wait()
    for copy in copies:
        copy.wait()

    squares = jnp.zeros((slots, 1), F32)
    total = jnp.zeros((slots, 3 * width), F32)
    for g in range(heads):
        x = gathered[g].astype(F32)
        squares = squares + jnp.sum(x * x, axis=1, keepdims=True)
        scaled = (x * gain_ref[:, g * width : (g + 1) * width]).astype(BF16)
        total = total + dot(scaled, wqkv[g * width : (g + 1) * width, :])
    proj[...] = (total * lax.rsqrt(squares / model + eps_norm)).astype(BF16)

    lane_col = iota((1, LANES), 1)
    context = []
    for pair in range(width // LANES):
        at = pair * LANES
        q2 = proj[:, at : at + LANES]
        k2 = proj[:, width + at : width + at + LANES]
        v2 = proj[:, 2 * width + at : 2 * width + at + LANES]
        mixed_heads = None
        for sub in range(LANES // HEAD_DIM):
            mine = (lane_col // HEAD_DIM) == sub
            q1 = jnp.where(mine, q2, jnp.zeros_like(q2))
            scores = (
                lax.dot_general(q1, k2, NT, preferred_element_type=F32)
                * (HEAD_DIM**-0.5)
                + bias
            )
            expo = jnp.exp(scores - jnp.max(scores, axis=1, keepdims=True))
            probs = (expo / jnp.sum(expo, axis=1, keepdims=True)).astype(BF16)
            out = dot(probs, v2)
            mixed_heads = out if sub == 0 else jnp.where(mine, out, mixed_heads)
        context.append(mixed_heads.astype(BF16))
    context = jnp.concatenate(context, axis=1)
    for g in range(heads):
        parts[g] = dot(context, wout[:, g * width : (g + 1) * width]).astype(BF16)
    copies = exchange(lambda t: parts.at[t], landed.at[head], 1)
    landed[head] = parts[head]
    for copy in copies:
        copy.wait()

    mixed = own[...].astype(F32)
    attended = landed[0].astype(F32)
    for g in range(1, heads):
        attended = attended + landed[g].astype(F32)
    mixed = mixed + attended
    encoded = mixed.astype(BF16).astype(F32)
    exact = lax.Precision.HIGHEST
    ones = jnp.ones((ROWS, width), F32)
    dotted = lax.dot_general(
        jnp.broadcast_to(sw_ref[...], (ROWS, width)),
        mixed,
        NT,
        precision=exact,
        preferred_element_type=F32,
    )
    squared = lax.dot_general(
        ones, mixed * mixed, NT, precision=exact, preferred_element_type=F32
    )
    stats[head] = jnp.where(iota((ROWS, slots), 0) == 0, dotted, squared)
    copies = exchange(lambda t: stats.at[head], stats.at[head], 2)
    for r in range(CAP):
        for half in range(2):
            wide[pl.ds(2 * r + half, shards, stride=ROWS), :] = encoded[
                r * shards : (r + 1) * shards, half * LANES : (half + 1) * LANES
            ]
    weight_row = jnp.zeros((1, slots), F32)
    for k in range(qw_ref.shape[1]):
        weight_row = weight_row + jnp.where(
            query_row == float(k + 1), qw_ref[0:1, k : k + 1], 0.0
        )
    for copy in copies:
        copy.wait()
    summed = stats[0]
    for g in range(1, heads):
        summed = summed + stats[g]
    score_row = summed[0:1, :] * lax.rsqrt(summed[1:2, :] / model + eps_norm)
    score_col = jnp.sum(jnp.where(diagonal, score_row, 0.0), axis=1, keepdims=True)

    above = grade_col - grade_row
    counted = jnp.where(
        related & (above != 0.0), jnp.where(above > 0.0, 1.0, -1.0), 0.0
    )
    spread = counted * (score_row - score_col)
    small = jnp.exp(-jnp.abs(spread))
    softplus = jnp.maximum(spread, 0.0) + jnp.log1p(small)
    sigmoid = jnp.where(spread >= 0.0, 1.0, small) / (1.0 + small)
    pull_row = weight_row * jnp.sum(counted * sigmoid, axis=0, keepdims=True)
    both = jnp.abs(counted)
    pair_row = weight_row * jnp.sum(both * softplus, axis=0, keepdims=True)
    pair_sum = 0.5 * jnp.sum(pair_row, axis=1, keepdims=True)
    pair_count = 0.5 * jnp.sum(
        jnp.sum(both, axis=0, keepdims=True), axis=1, keepdims=True
    )

    words = [score_row[:, r * shards : (r + 1) * shards] for r in range(CAP)]
    words += [pull_row[:, r * shards : (r + 1) * shards] for r in range(CAP)]
    words += [jnp.broadcast_to(v, (1, shards)) for v in (pair_sum, pair_count)]
    words = jnp.concatenate(words, axis=0)
    high = words.astype(BF16).astype(F32)
    middle = (words - high).astype(BF16).astype(F32)
    low = words - high - middle
    pieces = jnp.concatenate(
        [high, middle, low, jnp.zeros((LANES - 3 * ROWS, shards), F32)], axis=0
    )
    wide[pl.ds(2 * CAP, shards, stride=ROWS), :] = pieces.T
    wide[pl.ds(2 * CAP + 1, shards, stride=ROWS), :] = jnp.zeros((shards, LANES), F32)
    back_send[...] = wide[...].reshape(shards, ROWS, LANES).astype(BF16)

    def push_back(i, carry):
        pltpu.make_async_remote_copy(
            back_send.at[i],
            back.at[i],
            send_sem.at[1],
            recv_sem.at[1],
            device_id={"shard": peer(shards - i)},
            device_id_type=MESH,
        ).start()
        return carry

    lax.fori_loop(1, shards, push_back, 0)
    back[0] = back_send[0]
    others = back.at[pl.ds(1, shards - 1)]
    pltpu.make_async_copy(others, others, recv_sem.at[1]).wait()

    wide[...] = back[...].astype(F32).reshape(shards * ROWS, LANES)
    landed_rows = wide[...].astype(BF16)
    for half in range(2):
        enc_ref[:, half * LANES : (half + 1) * LANES] = lax.dot_general(
            place[half], landed_rows, TN, preferred_element_type=F32
        ).astype(BF16)
    pieces = rows_of(2 * CAP)
    sums = jnp.sum(pieces, axis=0, keepdims=True)
    sums = sums + pltpu.roll(sums, LANES - ROWS, 1) + pltpu.roll(sums, LANES - 2 * ROWS, 1)
    pair_total = jnp.maximum(sums[:, 7:8], 1.0)
    found = lax.dot_general(
        pieces.astype(BF16), named_f.astype(BF16), TN, preferred_element_type=F32
    )
    found = found[0:ROWS] + found[ROWS : 2 * ROWS] + found[2 * ROWS : 3 * ROWS]
    score_out = jnp.zeros((1, docs), F32)
    grad_out = jnp.zeros((1, docs), F32)
    for r in range(CAP):
        score_out = score_out + jnp.where(rank == r, found[r : r + 1], 0.0)
        grad_out = grad_out + jnp.where(rank == r, found[CAP + r : CAP + r + 1], 0.0)
    small_ref[0:1, :] = score_out
    small_ref[1:2, :] = grad_out / pair_total
    small_ref[2:3, :] = jnp.broadcast_to(sums[:, 6:7] / pair_total, (1, docs))
    small_ref[3:8, :] = jnp.zeros((5, docs), F32)

    for ref, at in ((send, 0), (back_send, 1)):
        sent = ref.at[pl.ds(1, shards - 1)]
        pltpu.make_async_copy(sent, sent, send_sem.at[at]).wait()


def body(
    features,
    owners,
    query_local,
    grades,
    query_weight,
    norm_gain,
    qkv_weight,
    out_weight,
    score_weight,
):
    shards = lax.axis_size("shard")
    heads = lax.axis_size("head")
    docs = features.shape[0]
    width, model = out_weight.shape
    slots = CAP * shards
    facts = jnp.stack([owners[:, 0], query_local, grades])
    vmem = pl.BlockSpec(memory_space=pltpu.VMEM)
    hbm = pl.BlockSpec(memory_space=pl.ANY)
    dma = pltpu.SemaphoreType.DMA
    blocks = pltpu.VMEM((shards, ROWS, LANES), BF16)
    encoded, small = pl.pallas_call(
        functools.partial(layer_kernel, shards, heads),
        out_shape=(
            jax.ShapeDtypeStruct((docs, width), BF16),
            jax.ShapeDtypeStruct((ROWS, docs), F32),
        ),
        in_specs=[vmem, vmem, vmem, vmem, hbm, hbm, vmem],
        out_specs=(vmem, vmem),
        scratch_shapes=[
            pltpu.VMEM((model, 3 * width), BF16),
            pltpu.VMEM((width, model), BF16),
            blocks,
            blocks,
            pltpu.VMEM((shards * ROWS, LANES), F32),
            pltpu.VMEM((heads, slots, width), BF16),
            pltpu.VMEM((slots, 3 * width), BF16),
            pltpu.VMEM((heads, slots, width), BF16),
            pltpu.VMEM((heads, slots, width), BF16),
            pltpu.VMEM((heads, ROWS, slots), F32),
            blocks,
            blocks,
            dma((2,)),
            dma((2,)),
            dma((2,)),
            dma((3, heads)),
            dma((3, heads)),
        ],
        compiler_params=pltpu.CompilerParams(
            collective_id=0, has_side_effects=True, vmem_limit_bytes=48 << 20
        ),
    )(
        features,
        facts,
        query_weight.reshape(1, -1),
        norm_gain.reshape(1, -1),
        qkv_weight.reshape(model, 3 * width),
        out_weight,
        score_weight.reshape(1, -1),
    )
    return encoded, small[0], small[1], small[2, 0]


def solution(mesh):
    placed = (
        P("shard", None),
        P("shard", None),
        P("shard"),
        P("shard"),
        P("shard"),
        P(),
        P(None, None, "head"),
        P("head", None),
        P("head"),
    )
    return jax.shard_map(
        body,
        mesh=mesh,
        in_specs=placed,
        out_specs=(P("shard", "head"), P("shard"), P("shard"), P()),
        check_vma=False,
    )
```

time: 470 us -> 91.8 us (0.20)
  blocking collectives: 258 us -> 0 us
  waiting for transfers between devices: 121 us -> 0 us
  Pallas kernels: 0 us -> 84.7 us
  starting transfers between devices: 41.6 us -> 0 us
  between operations: 16.8 us -> 0.76 us
  local copies, waits for them, and re-layouts: 16.5 us -> 6.16 us
  other arithmetic: 7.98 us -> 0.01 us
  matrix products: 6.75 us -> 0 us
    psum x2 -> x0, blocking collectives: 258 us -> none  [the longest x1 252 us: body(): total_sum, total_count = lax.psum((pair_sum, pair_count), 'shard')]
    all_to_all x4 -> x0, waiting for transfers between devices: 99.4 us -> none  [the longest x1 51.4 us: body(): lax.all_to_all(send_rows, 'shard', split_axis=0, concat_axis=0, tiled=True)]
    pallas_call x0 -> x1, Pallas kernels: none -> 84.7 us  [body(): pl.pallas_call(functools.partial(layer_kernel, shards, heads), out_shape=...]
    all_to_all x4 -> x0, starting transfers between devices: 41.4 us -> none  [the longest x1 20.4 us: body(): lax.all_to_all(send_meta, 'shard', split_axis=0, concat_axis=0, tiled=True)]
    reduce_scatter x1 -> x0, waiting for transfers between devices: 21.8 us -> none  [body(): lax.psum_scatter(partial_out.astype(jnp.bfloat16), 'head', scatter_dimens...]
    dot_general x4 -> x0, matrix products: 5.81 us -> none  [the longest x1 2.22 us: body(): jnp.dot(normed, qkv_weight.reshape(model_width, 3 * local_width), preferr...]
  transfers between devices with their start and end apart: 5 -> 0, of which waited for: 5 -> 0; matrix products, arithmetic and copies ran while one was open for 1% -> 0% of each run, Pallas kernels for 0% -> 0%
where the time goes in v2:
time: 91.8 us; the launch traced here: 91.6 us
  Pallas kernels  84.7 us (92%)
  local copies, waits for them, and re-layouts  6.16 us (7%)
    pallas_call x1, Pallas kernels, body(): pl.pallas_call(functools.partial(layer_kernel, shards, heads), out_shape=...  84.7 us
    unnamed x18, local copies, waits for them, and re-layouts  3.28 us

profile of v2, /device:TPU:1, one launch (start us, length us, event | category | flops | bytes accessed | tf_op | source)
XLA Modules:
  0.0 91.6 jit_solution(2421829778834090338)
XLA Ops:
  0.6 2.6 %copy.14 = bf16[1024,3,256]{0,2,1:T(8,128)(2,1)} copy(bf16[1024,3,256]{2,0,1:T(8,128)(2,1)} %param.15) | data formatting | bytes 3145728 | tf_op args[6]
  3.2 0.0 copy-start.5
  3.2 0.0 copy-start.6
  3.2 0.0 copy-start.7
  3.2 0.0 copy-start
  3.2 0.0 copy-start.1
  3.2 0.0 copy-start.2
  3.3 0.0 copy-start.3
  3.3 0.0 copy-start.4
  3.3 1.8 %copy.15.wqkv_hbm = bf16[1024,768]{1,0:T(8,128)(2,1)S(1)} copy(bf16[1024,768]{0,1:T(8,128)(2,1)} %bitcast.13) | data formatting | bytes 3145728 | tf_op jit(solution)/shard_map/reshape | solution.py:389
  5.1 0.0 copy-done.5
  5.1 0.0 copy-done.6
  5.1 0.0 copy-done.7
  5.1 0.0 copy-done
  5.1 0.0 copy-done.1
  5.1 0.0 copy-done.2
  5.2 0.0 copy-done.3
  5.2 0.0 copy-done.4
  5.2 84.7 %shard_map.120 = (bf16[256,256]{1,0:T(8,128)(2,1)S(1)}, f32[8,256]{1,0:T(8,128)S(1)}) custom-call(bf16[256,1024]{1,0:T(8,128)(2,1)S(1)} %copy-done, s32[3,256]{1,0:T(4,128)S(1)} %pad_add_fusion.doc_ref, f32[1,16]{1,0:T(1,128)S(1)} %bitcast.12, f32[1,1024]{1,0:T(1,128)S(1)} %bitcast.10, bf16[1024,768]{1,0:T(8,128)(2,1)S(1)} %copy.15.wqkv_hbm, ...), custom_call_target="tpu_custom_call" | custom-call | tf_op jit(solution)/shard_map/pallas_call | solution.py:354
  89.9 0.6 fusion
  90.5 0.5 slice.11
  91.0 0.7 copy.17
  (1 shorter events, 0.0 us)
Async XLA Ops:
  3.2 1.9 %copy-start.5 = (s32[256]{0:T(256)S(1)}, s32[256]{0:T(256)}, u32[]{:S(2)}) copy-start(s32[256]{0:T(256)} %param.12) | copy-start | bytes 3076
  3.2 1.9 %copy-start.6 = (s32[256]{0:T(256)S(1)}, s32[256]{0:T(256)}, u32[]{:S(2)}) copy-start(s32[256]{0:T(256)} %param.11) | copy-start | bytes 3076
  3.2 1.9 %copy-start.7 = (s32[256,1]{0,1:T(1,128)S(1)}, s32[256,1]{0,1:T(1,128)}, u32[]{:S(2)}) copy-start(s32[256,1]{0,1:T(1,128)} %param.10) | copy-start | bytes 3076
  3.2 1.9 %copy-start = (bf16[256,1024]{1,0:T(8,128)(2,1)S(1)}, bf16[256,1024]{1,0:T(8,128)(2,1)}, u32[]{:S(2)}) copy-start(bf16[256,1024]{1,0:T(8,128)(2,1)} %feat_ref.1) | copy-start | bytes 1572868
  3.2 1.9 %copy-start.1 = (bf16[256,1024]{1,0:T(8,128)(2,1)S(1)}, bf16[256,1024]{1,0:T(8,128)(2,1)}, u32[]{:S(2)}) copy-start(bf16[256,1024]{1,0:T(8,128)(2,1)} %wout_hbm.1) | copy-start | bytes 1572868
  3.2 1.9 %copy-start.2 = (f32[1024]{0:T(1024)S(1)}, f32[1024]{0:T(1024)}, u32[]{:S(2)}) copy-start(f32[1024]{0:T(1024)} %param.14) | copy-start | bytes 12292
  3.3 1.9 %copy-start.3 = (f32[256]{0:T(256)S(1)}, f32[256]{0:T(256)}, u32[]{:S(2)}) copy-start(f32[256]{0:T(256)} %param.17) | copy-start | bytes 3076
  3.3 1.9 %copy-start.4 = (f32[16]{0:T(128)S(1)}, f32[16]{0:T(128)}, u32[]{:S(2)}) copy-start(f32[16]{0:T(128)} %param.13) | copy-start | bytes 196

commit v3 on v2

v3 whole, which is shorter than its diff:
```python
import functools

import jax
import jax.numpy as jnp
from jax import lax
from jax.experimental import pallas as pl
from jax.experimental.pallas import tpu as pltpu
from jax.sharding import PartitionSpec as P

MESH = pl.DeviceIdType.MESH
HEAD_DIM = 64
CAP = 3
ROWS = 8
GROUPS = 4
LANES = 128
eps_norm = 1e-06
F32 = jnp.float32
BF16 = jnp.bfloat16
NT = (((1,), (1,)), ((), ()))
TN = (((0,), (0,)), ((), ()))


def dot(a, b):
    return jnp.dot(a, b, preferred_element_type=F32)


def iota(shape, dim):
    return lax.broadcasted_iota(jnp.int32, shape, dim)


def layer_kernel(
    shards,
    heads,
    feat_ref,
    doc_ref,
    qw_ref,
    gain_ref,
    wqkv_hbm,
    wout_hbm,
    sw_ref,
    enc_ref,
    small_ref,
    wqkv,
    wout,
    sw_all,
    send,
    recv,
    wide,
    gathered,
    proj,
    context,
    mixed_ref,
    back_send,
    back,
    score_send,
    score_recv,
    local_sem,
    send_sem,
    recv_sem,
    y_send,
    y_recv,
    pair_send,
    pair_recv,
):
    me = lax.axis_index("shard")
    head = lax.axis_index("head")
    docs = feat_ref.shape[0]
    width = wout_hbm.shape[0]
    model = wout_hbm.shape[1]
    slots = CAP * shards
    group = shards // GROUPS
    rows = CAP * group

    def peer(i):
        return lax.rem(me + i, shards)

    def head_peer(i):
        return lax.rem(head + i, heads)

    barrier = pltpu.get_barrier_semaphore()

    def greet(i, carry):
        pl.semaphore_signal(
            barrier, 1, device_id={"shard": peer(i)}, device_id_type=MESH
        )
        return carry

    lax.fori_loop(1, shards, greet, 0)
    for i in range(1, heads):
        pl.semaphore_signal(
            barrier, 1, device_id={"head": head_peer(i)}, device_id_type=MESH
        )
    load_qkv = pltpu.make_async_copy(wqkv_hbm, wqkv, local_sem.at[0])
    load_out = pltpu.make_async_copy(wout_hbm, wout.at[head], local_sem.at[1])
    load_qkv.start()
    load_out.start()

    owner = jnp.bitwise_and(doc_ref[0:1, :] - me, shards - 1)
    query = doc_ref[1:2, :].astype(F32) + 1.0
    grade = doc_ref[2:3, :].astype(F32)
    named = iota((shards, docs), 0) == owner
    named_f = named.astype(F32)
    earlier = (iota((docs, docs), 0) < iota((docs, docs), 1)).astype(F32).astype(BF16)
    before = dot(named_f.astype(BF16), earlier)
    rank_f = jnp.sum(before * named_f, axis=0, keepdims=True)
    rank = rank_f.astype(jnp.int32)
    first = owner * ROWS + 2 * rank
    block_row = iota((shards * ROWS, docs), 0)
    place = [
        (block_row == where).astype(F32).astype(BF16)
        for where in (first, first + 1, owner * ROWS + 2 * CAP)
    ]
    lane = iota((LANES, docs), 0)
    facts = jnp.where(lane == rank, query, 0.0) + jnp.where(
        lane == rank + CAP, grade, 0.0
    )
    left = pl.ds(pl.multiple_of(head * width, LANES), LANES)
    right = pl.ds(pl.multiple_of(head * width + LANES, LANES), LANES)
    block = dot(place[0], feat_ref[:, left]) + dot(place[1], feat_ref[:, right])
    block = block + lax.dot_general(
        place[2], facts.astype(BF16), NT, preferred_element_type=F32
    )
    send[...] = block.reshape(shards, ROWS, LANES).astype(BF16)
    sw_all[head] = jnp.broadcast_to(sw_ref[...], (ROWS, width))

    def exchange(source, target, step):
        copies = []
        for i in (2, 1, 3):
            copy = pltpu.make_async_remote_copy(
                source,
                target,
                y_send.at[step, i],
                y_recv.at[step, i],
                device_id={"head": head_peer(i)},
                device_id_type=MESH,
            )
            copy.start()
            copies.append(copy)
        return copies

    core = lax.rem(me, 2)
    half_rows = width // 2
    half = pl.ds(pl.multiple_of(core * half_rows, half_rows), half_rows)

    pl.semaphore_wait(barrier, shards - 1 + heads - 1)

    out_copies = exchange(wout_hbm.at[half], wout.at[head, half], 2 * GROUPS)
    sw_copies = exchange(sw_all.at[head], sw_all.at[head], 2 * GROUPS + 1)

    for g in range(GROUPS):

        def push(i, carry, g=g):
            pltpu.make_async_remote_copy(
                send.at[i],
                recv.at[i],
                send_sem.at[0],
                recv_sem.at[g],
                device_id={"shard": peer(i)},
                device_id_type=MESH,
            ).start()
            return carry

        lax.fori_loop(max(1, g * group), (g + 1) * group, push, 0)
    recv[0] = send[0]

    def arrived(ref, sem, g):
        low = max(1, g * group)
        some = ref.at[pl.ds(low, (g + 1) * group - low)]
        pltpu.make_async_copy(some, some, sem).wait()

    load_qkv.wait()
    load_out.wait()

    def slots_of(g):
        return pl.ds(g * rows, rows)

    def project(g, copies):
        for copy in copies:
            copy.wait()
        squares = jnp.zeros((rows, 1), F32)
        total = [jnp.zeros((rows, width), F32) for _ in range(3)]
        for k in range(heads):
            x = gathered[k, slots_of(g), :].astype(F32)
            squares = squares + jnp.sum(x * x, axis=1, keepdims=True)
            scaled = (x * gain_ref[:, k * width : (k + 1) * width]).astype(BF16)
            for j in range(3):
                total[j] = total[j] + dot(scaled, wqkv[j, k * width : (k + 1) * width])
        scale = lax.rsqrt(squares / model + eps_norm)
        for j in range(3):
            proj[slots_of(g), j * width : (j + 1) * width] = (
                total[j] * scale
            ).astype(BF16)

    fact_cols = []
    copies = []
    for g in range(GROUPS):
        arrived(recv, recv_sem.at[g], g)
        wide[...] = (
            recv[pl.ds(g * group, group)].astype(F32).reshape(group * ROWS, LANES)
        )
        for r in range(CAP):
            for k in range(2):
                gathered[
                    head,
                    g * rows + r * group : g * rows + (r + 1) * group,
                    k * LANES : (k + 1) * LANES,
                ] = wide[pl.ds(2 * r + k, group, stride=ROWS), :].astype(BF16)
        own = gathered.at[head, slots_of(g)]
        copies.append(exchange(own, own, g))
        fact_cols.append(wide[pl.ds(2 * CAP, group, stride=ROWS), :])
        if g >= 2:
            project(g - 2, copies[g - 2])

    diagonal = iota((slots, slots), 0) == iota((slots, slots), 1)

    def column(at):
        return jnp.concatenate(
            [f[:, at + r : at + r + 1] for f in fact_cols for r in range(CAP)], axis=0
        )

    def to_row(col):
        return jnp.sum(jnp.where(diagonal, col, 0.0), axis=0, keepdims=True)

    query_col, grade_col = column(0), column(CAP)
    query_row, grade_row = to_row(query_col), to_row(grade_col)
    related = (query_col == query_row) & (query_col > 0.5)
    bias = jnp.where(related | diagonal, 0.0, -jnp.inf)
    above = grade_col - grade_row
    counted = jnp.where(
        related & (above != 0.0), jnp.where(above > 0.0, 1.0, -1.0), 0.0
    )
    weight_col = jnp.zeros((slots, 1), F32)
    for k in range(qw_ref.shape[1]):
        weight_col = weight_col + jnp.where(
            query_col == float(k + 1), qw_ref[0:1, k : k + 1], 0.0
        )
    project(GROUPS - 2, copies[GROUPS - 2])

    for copy in out_copies + sw_copies:
        copy.wait()
    pair_copies = []
    for i in range(1, heads):
        piece = wout.at[lax.rem(head + heads - i, heads), half]
        copy = pltpu.make_async_remote_copy(
            piece,
            piece,
            pair_send.at[i],
            pair_recv.at[i],
            device_id={"shard": me + 1 - 2 * core},
            device_id_type=MESH,
        )
        copy.start()
        pair_copies.append(copy)
    project(GROUPS - 1, copies[GROUPS - 1])

    lane_col = iota((1, LANES), 1)
    copies = []
    for g in range(GROUPS):
        for pair in range(width // LANES):
            at = pair * LANES
            q2 = proj[slots_of(g), at : at + LANES]
            k2 = proj[:, width + at : width + at + LANES]
            v2 = proj[:, 2 * width + at : 2 * width + at + LANES]
            both_heads = None
            for sub in range(LANES // HEAD_DIM):
                mine = (lane_col // HEAD_DIM) == sub
                q1 = jnp.where(mine, q2, jnp.zeros_like(q2))
                scores = (
                    lax.dot_general(q1, k2, NT, preferred_element_type=F32)
                    * (HEAD_DIM**-0.5)
                    + bias[g * rows : (g + 1) * rows, :]
                )
                expo = jnp.exp(scores - jnp.max(scores, axis=1, keepdims=True))
                probs = (expo / jnp.sum(expo, axis=1, keepdims=True)).astype(BF16)
                out = dot(probs, v2)
                both_heads = out if sub == 0 else jnp.where(mine, out, both_heads)
            context[head, slots_of(g), at : at + LANES] = both_heads.astype(BF16)
        own = context.at[head, slots_of(g)]
        copies.append(exchange(own, own, GROUPS + g))
    for copy in pair_copies:
        copy.wait()

    own_cols = pl.ds(pl.multiple_of(head * width, width), width)
    score_cols = []
    for g in range(GROUPS):
        for copy in copies[g]:
            copy.wait()
        attended = dot(context[0, slots_of(g), :], wout[0])
        for k in range(1, heads):
            attended = attended + dot(context[k, slots_of(g), :], wout[k])
        squares = jnp.zeros((rows, 1), F32)
        weighted = jnp.zeros((rows, 1), F32)
        for k in range(heads):
            mixed = (
                gathered[k, slots_of(g), :].astype(F32)
                + attended[:, k * width : (k + 1) * width]
            )
            mixed_ref[:, k * width : (k + 1) * width] = mixed
            squares = squares + jnp.sum(mixed * mixed, axis=1, keepdims=True)
            weighted = weighted + jnp.sum(
                mixed * sw_all[k, 0:1, :], axis=1, keepdims=True
            )
        score_cols.append(weighted * lax.rsqrt(squares / model + eps_norm))
        encoded = mixed_ref[:, own_cols]
        for r in range(CAP):
            for k in range(2):
                wide[pl.ds(2 * r + k, group, stride=ROWS), :] = encoded[
                    r * group : (r + 1) * group, k * LANES : (k + 1) * LANES
                ]
        for k in range(2 * CAP, ROWS):
            wide[pl.ds(k, group, stride=ROWS), :] = jnp.zeros((group, LANES), F32)
        back_send[pl.ds(g * group, group)] = (
            wide[...].reshape(group, ROWS, LANES).astype(BF16)
        )

        def push_back(i, carry, g=g):
            pltpu.make_async_remote_copy(
                back_send.at[i],
                back.at[i],
                send_sem.at[1],
                recv_sem.at[GROUPS + g],
                device_id={"shard": peer(shards - i)},
                device_id_type=MESH,
            ).start()
            return carry

        lax.fori_loop(max(1, g * group), (g + 1) * group, push_back, 0)
    back[0] = back_send[0]

    score_col = jnp.concatenate(score_cols, axis=0)
    spread = counted * (to_row(score_col) - score_col)
    small = jnp.exp(-jnp.abs(spread))
    softplus = jnp.maximum(spread, 0.0) + jnp.log1p(small)
    sigmoid = jnp.where(spread >= 0.0, 1.0, small) / (1.0 + small)
    both = jnp.abs(counted)
    pull_col = -weight_col * jnp.sum(counted * sigmoid, axis=1, keepdims=True)
    pair_col = weight_col * jnp.sum(both * softplus, axis=1, keepdims=True)
    pair_sum = 0.5 * jnp.sum(pair_col, axis=0, keepdims=True)
    pair_count = 0.5 * jnp.sum(
        jnp.sum(both, axis=1, keepdims=True), axis=0, keepdims=True
    )

    def by_source(col, r):
        return jnp.concatenate(
            [
                col[g * rows + r * group : g * rows + (r + 1) * group]
                for g in range(GROUPS)
            ],
            axis=0,
        )

    words = [by_source(score_col, r) for r in range(CAP)]
    words += [by_source(pull_col, r) for r in range(CAP)]
    words += [pair_sum, pair_count]
    message = jnp.zeros((shards, LANES), F32)
    for k, word in enumerate(words):
        message = jnp.where(lane_col == k, word, message)
    score_send[...] = message.reshape(shards, 1, LANES)

    def push_scores(i, carry):
        pltpu.make_async_remote_copy(
            score_send.at[i],
            score_recv.at[i],
            send_sem.at[2],
            recv_sem.at[2 * GROUPS],
            device_id={"shard": peer(shards - i)},
            device_id_type=MESH,
        ).start()
        return carry

    lax.fori_loop(1, shards, push_scores, 0)
    score_recv[0] = score_send[0]

    placed = [jnp.zeros((docs, LANES), F32) for _ in range(2)]
    for g in range(GROUPS):
        arrived(back, recv_sem.at[GROUPS + g], g)
        landed = (
            back[pl.ds(g * group, group)]
            .astype(F32)
            .reshape(group * ROWS, LANES)
            .astype(BF16)
        )
        for k in range(2):
            placed[k] = placed[k] + lax.dot_general(
                place[k][g * group * ROWS : (g + 1) * group * ROWS],
                landed,
                TN,
                preferred_element_type=F32,
            )
    for k in range(2):
        enc_ref[:, k * LANES : (k + 1) * LANES] = placed[k].astype(BF16)
    others = score_recv.at[pl.ds(1, shards - 1)]
    pltpu.make_async_copy(others, others, recv_sem.at[2 * GROUPS]).wait()
    message = score_recv[...].reshape(shards, LANES)
    sums = jnp.sum(message, axis=0, keepdims=True)
    pair_total = jnp.maximum(sums[:, 7:8], 1.0)
    found = lax.dot_general(
        message,
        named_f,
        TN,
        precision=lax.Precision.HIGHEST,
        preferred_element_type=F32,
    )
    score_out = jnp.zeros((1, docs), F32)
    grad_out = jnp.zeros((1, docs), F32)
    for r in range(CAP):
        score_out = score_out + jnp.where(rank == r, found[r : r + 1], 0.0)
        grad_out = grad_out + jnp.where(rank == r, found[CAP + r : CAP + r + 1], 0.0)
    small_ref[0:1, :] = score_out
    small_ref[1:2, :] = grad_out / pair_total
    small_ref[2:3, :] = jnp.broadcast_to(sums[:, 6:7] / pair_total, (1, docs))
    small_ref[3:8, :] = jnp.zeros((5, docs), F32)

    for at, ref in enumerate((send, back_send, score_send)):
        sent = ref.at[pl.ds(1, shards - 1)]
        pltpu.make_async_copy(sent, sent, send_sem.at[at]).wait()


def body(
    features,
    owners,
    query_local,
    grades,
    query_weight,
    norm_gain,
    qkv_weight,
    out_weight,
    score_weight,
):
    shards = lax.axis_size("shard")
    heads = lax.axis_size("head")
    docs = features.shape[0]
    width, model = out_weight.shape
    slots = CAP * shards
    facts = jnp.stack([owners[:, 0], query_local, grades])
    vmem = pl.BlockSpec(memory_space=pltpu.VMEM)
    hbm = pl.BlockSpec(memory_space=pl.ANY)
    dma = pltpu.SemaphoreType.DMA
    blocks = pltpu.VMEM((shards, ROWS, LANES), BF16)
    encoded, small = pl.pallas_call(
        functools.partial(layer_kernel, shards, heads),
        out_shape=(
            jax.ShapeDtypeStruct((docs, width), BF16),
            jax.ShapeDtypeStruct((ROWS, docs), F32),
        ),
        in_specs=[vmem, vmem, vmem, vmem, hbm, hbm, vmem],
        out_specs=(vmem, vmem),
        scratch_shapes=[
            pltpu.VMEM((3, model, width), BF16),
            pltpu.VMEM((heads, width, model), BF16),
            pltpu.VMEM((heads, ROWS, width), F32),
            blocks,
            blocks,
            pltpu.VMEM((shards * ROWS // GROUPS, LANES), F32),
            pltpu.VMEM((heads, slots, width), BF16),
            pltpu.VMEM((slots, 3 * width), BF16),
            pltpu.VMEM((heads, slots, width), BF16),
            pltpu.VMEM((slots // GROUPS, model), F32),
            blocks,
            blocks,
            pltpu.VMEM((shards, 1, LANES), F32),
            pltpu.VMEM((shards, 1, LANES), F32),
            dma((2,)),
            dma((3,)),
            dma((2 * GROUPS + 1,)),
            dma((2 * GROUPS + 2, heads)),
            dma((2 * GROUPS + 2, heads)),
            dma((heads,)),
            dma((heads,)),
        ],
        compiler_params=pltpu.CompilerParams(
            collective_id=0, has_side_effects=True, vmem_limit_bytes=48 << 20
        ),
    )(
        features,
        facts,
        query_weight.reshape(1, -1),
        norm_gain.reshape(1, -1),
        jnp.transpose(qkv_weight, (1, 0, 2)),
        out_weight,
        score_weight.reshape(1, -1),
    )
    return encoded, small[0], small[1], small[2, 0]


def solution(mesh):
    placed = (
        P("shard", None),
        P("shard", None),
        P("shard"),
        P("shard"),
        P("shard"),
        P(),
        P(None, None, "head"),
        P("head", None),
        P("head"),
    )
    return jax.shard_map(
        body,
        mesh=mesh,
        in_specs=placed,
        out_specs=(P("shard", "head"), P("shard"), P("shard"), P()),
        check_vma=False,
    )
```

time: 91.8 us -> 79.9 us (0.87)
  Pallas kernels: 84.7 us -> 70.9 us
  local copies, waits for them, and re-layouts: 6.16 us -> 7.25 us
    pallas_call x1, Pallas kernels: 84.7 us -> 70.9 us  [body(): pl.pallas_call(functools.partial(layer_kernel, shards, heads), out_shape=...]
    unnamed x18 -> x13, local copies, waits for them, and re-layouts: 3.28 us -> 6.16 us
    reshape x1 -> x0, local copies, waits for them, and re-layouts: 1.8 us -> none  [body(): qkv_weight.reshape(model, 3 * width)]
where the time goes in v3:
time: 79.9 us; the launch traced here: 79.5 us
  Pallas kernels  70.9 us (89%)
  local copies, waits for them, and re-layouts  7.25 us (9%)
    pallas_call x1, Pallas kernels, body(): pl.pallas_call(functools.partial(layer_kernel, shards, heads), out_shape=...  70.9 us
    unnamed x13, local copies, waits for them, and re-layouts  6.16 us

profile of v3, /device:TPU:1, one launch (start us, length us, event | category | flops | bytes accessed | tf_op | source)
XLA Modules:
  0.0 79.5 jit_solution(12783603469317866985)
XLA Ops:
  0.6 0.7 pad_add_fusion.doc_ref
  1.4 0.0 copy-start
  1.4 1.4 %copy-done = bf16[1024,3,256]{2,0,1:T(8,128)(2,1)S(1)} copy-done((bf16[1024,3,256]{2,0,1:T(8,128)(2,1)S(1)}, bf16[1024,3,256]{2,0,1:T(8,128)(2,1)}, u32[]{:S(2)}) %copy-start) | copy-done | bytes 1572888
  2.8 0.0 copy-start.1
  2.8 1.0 %copy-done.1 = bf16[256,1024]{1,0:T(8,128)(2,1)S(1)} copy-done((bf16[256,1024]{1,0:T(8,128)(2,1)S(1)}, bf16[256,1024]{1,0:T(8,128)(2,1)}, u32[]{:S(2)}) %copy-start.1) | copy-done | bytes 524312
  3.8 0.0 copy-start.2
  3.8 1.0 %copy-done.2 = bf16[256,1024]{1,0:T(8,128)(2,1)S(1)} copy-done((bf16[256,1024]{1,0:T(8,128)(2,1)S(1)}, bf16[256,1024]{1,0:T(8,128)(2,1)}, u32[]{:S(2)}) %copy-start.2) | copy-done | bytes 524312
  4.8 0.0 copy-start.3
  4.8 0.7 copy-done.3
  5.5 0.0 copy-start.4
  5.5 0.7 copy-done.4
  6.2 0.0 copy-start.5
  6.2 0.7 copy-done.5
  6.9 70.9 %shard_map.120 = (bf16[256,256]{1,0:T(8,128)(2,1)S(1)}, f32[8,256]{1,0:T(8,128)S(1)}) custom-call(bf16[256,1024]{1,0:T(8,128)(2,1)S(1)} %copy-done.1, s32[3,256]{1,0:T(4,128)S(1)} %pad_add_fusion.doc_ref, f32[1,16]{1,0:T(1,128)S(1)} %bitcast.13, f32[1,1024]{1,0:T(1,128)S(1)} %bitcast.11, bf16[3,1024,256]{2,1,0:T(8,128)(2,1)S(1)} %bitcast.10, ...), custom_call_target="tpu_custom_call" | custom-call | tf_op jit(solution)/shard_map/pallas_call | solution.py:440
  77.8 0.6 fusion
  78.4 0.5 slice.11
  78.9 0.7 copy.14
Async XLA Ops:
  1.4 1.4 %copy-start = (bf16[1024,3,256]{2,0,1:T(8,128)(2,1)S(1)}, bf16[1024,3,256]{2,0,1:T(8,128)(2,1)}, u32[]{:S(2)}) copy-start(bf16[1024,3,256]{2,0,1:T(8,128)(2,1)} %param.15) | copy-start | bytes 4718596
  2.8 1.0 %copy-start.1 = (bf16[256,1024]{1,0:T(8,128)(2,1)S(1)}, bf16[256,1024]{1,0:T(8,128)(2,1)}, u32[]{:S(2)}) copy-start(bf16[256,1024]{1,0:T(8,128)(2,1)} %feat_ref.1) | copy-start | bytes 1572868
  3.8 1.0 %copy-start.2 = (bf16[256,1024]{1,0:T(8,128)(2,1)S(1)}, bf16[256,1024]{1,0:T(8,128)(2,1)}, u32[]{:S(2)}) copy-start(bf16[256,1024]{1,0:T(8,128)(2,1)} %wout_hbm.1) | copy-start | bytes 1572868
  4.8 0.7 copy-start.3
  5.5 0.7 copy-start.4
  6.2 0.7 copy-start.5

commit v4 on v3

v4 whole, which is shorter than its diff:
```python
import functools

import jax
import jax.numpy as jnp
from jax import lax
from jax.experimental import pallas as pl
from jax.experimental.pallas import tpu as pltpu
from jax.sharding import PartitionSpec as P

MESH = pl.DeviceIdType.MESH
HEAD_DIM = 64
CAP = 3
ROWS = 8
SIXTEENTHS = (4, 4, 4, 2, 2)
GROUPS = len(SIXTEENTHS)
LANES = 128
eps_norm = 1e-06
F32 = jnp.float32
BF16 = jnp.bfloat16
NT = (((1,), (1,)), ((), ()))
TN = (((0,), (0,)), ((), ()))


def dot(a, b):
    return jnp.dot(a, b, preferred_element_type=F32)


def iota(shape, dim):
    return lax.broadcasted_iota(jnp.int32, shape, dim)


def layer_kernel(
    shards,
    heads,
    query_count,
    feat_hbm,
    inputs_ref,
    wqkv_hbm,
    wout_hbm,
    enc_ref,
    small_ref,
    feat_ref,
    wqkv,
    wout,
    sw_all,
    send,
    recv,
    facts_send,
    facts_recv,
    spread_rows,
    gathered,
    proj,
    context,
    mixed_ref,
    back_send,
    back,
    score_send,
    score_recv,
    local_sem,
    send_sem,
    recv_sem,
    y_send,
    y_recv,
    pair_send,
    pair_recv,
    facts_sent,
    facts_came,
    facts_y_sent,
    facts_y_came,
):
    me = lax.axis_index("shard")
    head = lax.axis_index("head")
    docs = feat_hbm.shape[0]
    width = wout_hbm.shape[0]
    model = wout_hbm.shape[1]
    slots = CAP * shards
    cut = [shards * sum(SIXTEENTHS[:g]) // 16 for g in range(GROUPS + 1)]
    share = shards // heads

    def in_halves(x):
        return jnp.stack([x[:, :LANES], x[:, LANES:]], axis=1).astype(BF16)

    def halves_of(ref, g):
        x = ref[slots_of(g)].astype(F32)
        return [x[:, k, :].astype(BF16) for k in range(2)]

    def slots_of(g):
        return slice(cut[g] * CAP, cut[g + 1] * CAP)

    def peer(i):
        return lax.rem(me + i, shards)

    def head_peer(i):
        return lax.rem(head + i, heads)

    cols = pl.ds(pl.multiple_of(head * width, width), width)
    arguments = (
        (feat_hbm.at[:, cols], feat_ref),
        (wqkv_hbm, wqkv),
        (wout_hbm, wout.at[head]),
    )
    loads = [
        pltpu.make_async_copy(source, target, local_sem.at[k])
        for k, (source, target) in enumerate(arguments)
    ]
    for load in loads:
        load.start()

    barrier = pltpu.get_barrier_semaphore()

    def greet(i, carry):
        pl.semaphore_signal(
            barrier, 1, device_id={"shard": peer(i)}, device_id_type=MESH
        )
        return carry

    lax.fori_loop(1, shards, greet, 0, unroll=True)
    for i in range(1, heads):
        pl.semaphore_signal(
            barrier, 1, device_id={"head": head_peer(i)}, device_id_type=MESH
        )

    owner = jnp.bitwise_and(
        inputs_ref[0:1, :docs].astype(jnp.int32) - me, shards - 1
    )
    query = inputs_ref[1:2, :docs] + 1.0
    grade = inputs_ref[2:3, :docs]
    named = iota((shards, docs), 0) == owner
    named_f = named.astype(F32)
    earlier = (iota((docs, docs), 0) < iota((docs, docs), 1)).astype(F32).astype(BF16)
    before = dot(named_f.astype(BF16), earlier)
    rank_f = jnp.sum(before * named_f, axis=0, keepdims=True)
    rank = rank_f.astype(jnp.int32)
    place = (iota((slots, docs), 0) == owner * CAP + rank).astype(F32).astype(BF16)
    lane = iota((LANES, docs), 0)
    facts = jnp.where(lane == rank, query, 0.0) + jnp.where(
        lane == rank + CAP, grade, 0.0
    )
    loads[0].wait()
    block = dot(place, feat_ref[...])
    send[...] = in_halves(block)
    facts_send[...] = lax.dot_general(
        named_f.astype(BF16), facts.astype(BF16), NT, preferred_element_type=F32
    ).reshape(shards, 1, LANES)
    sw_all[head] = jnp.broadcast_to(inputs_ref[3:4, :width], (ROWS, width))

    def exchange(source, target, step):
        copies = []
        for i in (2, 1, 3):
            copy = pltpu.make_async_remote_copy(
                source,
                target,
                y_send.at[step, i],
                y_recv.at[step, i],
                device_id={"head": head_peer(i)},
                device_id_type=MESH,
            )
            copy.start()
            copies.append(copy)
        return copies

    core = lax.rem(me, 2)
    half_rows = width // 2
    half = pl.ds(pl.multiple_of(core * half_rows, half_rows), half_rows)

    pl.semaphore_wait(barrier, shards - 1 + heads - 1)

    out_copies = exchange(wout_hbm.at[half], wout.at[head, half], 2 * GROUPS)
    sw_copies = exchange(sw_all.at[head], sw_all.at[head], 2 * GROUPS + 1)

    def push_facts(i, carry):
        pltpu.make_async_remote_copy(
            facts_send.at[i],
            facts_recv.at[i],
            facts_sent,
            facts_came,
            device_id={"shard": peer(i)},
            device_id_type=MESH,
        ).start()
        return carry

    for g in range(heads):

        @pl.when(head == g)
        def _(g=g):
            lax.fori_loop(max(1, g * share), (g + 1) * share, push_facts, 0)

    for g in range(GROUPS):

        def push(i, carry, g=g):
            at = pl.ds(i * CAP, CAP)
            pltpu.make_async_remote_copy(
                send.at[at],
                recv.at[at],
                send_sem.at[0],
                recv_sem.at[g],
                device_id={"shard": peer(i)},
                device_id_type=MESH,
            ).start()
            return carry

        lax.fori_loop(max(1, cut[g]), cut[g + 1], push, 0)
    recv[0:CAP] = send[0:CAP]

    def arrived(ref, sem, g):
        low = max(1, cut[g]) * CAP
        some = ref.at[pl.ds(low, cut[g + 1] * CAP - low)]
        pltpu.make_async_copy(some, some, sem).wait()

    def share_facts(g):
        low = max(1, g * share)
        got = facts_recv.at[pl.ds(low, (g + 1) * share - low)]
        all_of = facts_recv.at[pl.ds(g * share, share)]
        mine = head == g

        def to(i):
            return pltpu.make_async_remote_copy(
                all_of,
                all_of,
                facts_y_sent.at[i],
                facts_y_came.at[g],
                device_id={"head": head_peer(i)},
                device_id_type=MESH,
            )

        @pl.when(mine)
        def _():
            if g == 0:
                facts_recv[0] = facts_send[0]
            pltpu.make_async_copy(got, got, facts_came).wait()
            for i in (2, 1, 3):
                to(i).start()

        def finish():
            @pl.when(mine)
            def _():
                for i in (2, 1, 3):
                    to(i).wait_send()
                sent = facts_send.at[pl.ds(low, (g + 1) * share - low)]
                pltpu.make_async_copy(sent, sent, facts_sent).wait()

            @pl.when(jnp.logical_not(mine))
            def _():
                to(1).wait_recv()

        return finish

    for load in loads[1:]:
        load.wait()

    def project(g, copies):
        for copy in copies:
            copy.wait()
        rows = (cut[g + 1] - cut[g]) * CAP
        squares = jnp.zeros((rows, 1), F32)
        total = [jnp.zeros((rows, width), F32) for _ in range(3)]
        for k in range(heads):
            x = gathered[k, slots_of(g), :].astype(F32)
            squares = squares + jnp.sum(x * x, axis=1, keepdims=True)
            scaled = (x * inputs_ref[4:5, k * width : (k + 1) * width]).astype(BF16)
            for j in range(3):
                total[j] = total[j] + dot(scaled, wqkv[j, k * width : (k + 1) * width])
        scale = lax.rsqrt(squares / model + eps_norm)
        for j in range(3):
            proj[slots_of(g), j * width : (j + 1) * width] = (
                total[j] * scale
            ).astype(BF16)

    copies = []
    finish_facts = [share_facts(g) for g in range(heads)]
    for g in range(GROUPS):
        arrived(recv, recv_sem.at[g], g)
        for k, part in enumerate(halves_of(recv, g)):
            gathered[head, slots_of(g), k * LANES : (k + 1) * LANES] = part
        own = gathered.at[head, slots_of(g)]
        copies.append(exchange(own, own, g))
        if g == 1:
            for finish in finish_facts:
                finish()
            lane_col = iota((1, LANES), 1)
            facts = facts_recv[...].reshape(shards, LANES)
            for r in range(CAP):
                spread_rows[pl.ds(r, shards, stride=CAP), :] = jnp.where(
                    lane_col == 0, facts[:, r : r + 1], facts[:, CAP + r : CAP + r + 1]
                )
            diagonal = iota((slots, slots), 0) == iota((slots, slots), 1)

            def to_row(col):
                return jnp.sum(jnp.where(diagonal, col, 0.0), axis=0, keepdims=True)

            query_col, grade_col = spread_rows[:, 0:1], spread_rows[:, 1:2]
            query_row, grade_row = to_row(query_col), to_row(grade_col)
            related = (query_col == query_row) & (query_col > 0.5)
            bias = jnp.where(related | diagonal, 0.0, -jnp.inf)
            above = grade_col - grade_row
            counted = jnp.where(
                related & (above != 0.0), jnp.where(above > 0.0, 1.0, -1.0), 0.0
            )
            weight_col = jnp.zeros((slots, 1), F32)
            for k in range(query_count):
                weight_col = weight_col + jnp.where(
                    query_col == float(k + 1), inputs_ref[5:6, k : k + 1], 0.0
                )
        if g >= 2:
            project(g - 2, copies[g - 2])
    project(GROUPS - 2, copies[GROUPS - 2])

    for copy in out_copies + sw_copies:
        copy.wait()
    pair_copies = []
    for i in range(1, heads):
        piece = wout.at[lax.rem(head + heads - i, heads), half]
        copy = pltpu.make_async_remote_copy(
            piece,
            piece,
            pair_send.at[i],
            pair_recv.at[i],
            device_id={"shard": me + 1 - 2 * core},
            device_id_type=MESH,
        )
        copy.start()
        pair_copies.append(copy)
    project(GROUPS - 1, copies[GROUPS - 1])

    copies = []
    for g in range(GROUPS):
        for pair in range(width // LANES):
            at = pair * LANES
            q2 = proj[slots_of(g), at : at + LANES]
            k2 = proj[:, width + at : width + at + LANES]
            v2 = proj[:, 2 * width + at : 2 * width + at + LANES]
            both_heads = None
            for sub in range(LANES // HEAD_DIM):
                mine = (lane_col // HEAD_DIM) == sub
                q1 = jnp.where(mine, q2, jnp.zeros_like(q2))
                scores = (
                    lax.dot_general(q1, k2, NT, preferred_element_type=F32)
                    * (HEAD_DIM**-0.5)
                    + bias[slots_of(g), :]
                )
                expo = jnp.exp(scores - jnp.max(scores, axis=1, keepdims=True))
                probs = (expo / jnp.sum(expo, axis=1, keepdims=True)).astype(BF16)
                out = dot(probs, v2)
                both_heads = out if sub == 0 else jnp.where(mine, out, both_heads)
            context[head, slots_of(g), at : at + LANES] = both_heads.astype(BF16)
        own = context.at[head, slots_of(g)]
        copies.append(exchange(own, own, GROUPS + g))
    for copy in pair_copies:
        copy.wait()

    score_cols = []
    for g in range(GROUPS):
        for copy in copies[g]:
            copy.wait()
        attended = dot(context[0, slots_of(g), :], wout[0])
        for k in range(1, heads):
            attended = attended + dot(context[k, slots_of(g), :], wout[k])
        rows = (cut[g + 1] - cut[g]) * CAP
        squares = jnp.zeros((rows, 1), F32)
        weighted = jnp.zeros((rows, 1), F32)
        for k in range(heads):
            mixed = (
                gathered[k, slots_of(g), :].astype(F32)
                + attended[:, k * width : (k + 1) * width]
            )
            mixed_ref[0:rows, k * width : (k + 1) * width] = mixed
            squares = squares + jnp.sum(mixed * mixed, axis=1, keepdims=True)
            weighted = weighted + jnp.sum(
                mixed * sw_all[k, 0:1, :], axis=1, keepdims=True
            )
        score_cols.append(weighted * lax.rsqrt(squares / model + eps_norm))
        back_send[slots_of(g)] = in_halves(mixed_ref[0:rows, cols])

        def push_back(i, carry, g=g):
            at = pl.ds(i * CAP, CAP)
            pltpu.make_async_remote_copy(
                back_send.at[at],
                back.at[at],
                send_sem.at[1],
                recv_sem.at[GROUPS + g],
                device_id={"shard": peer(shards - i)},
                device_id_type=MESH,
            ).start()
            return carry

        lax.fori_loop(
            max(1, cut[g]), cut[g + 1], push_back, 0, unroll=g == GROUPS - 1
        )
    back[0:CAP] = back_send[0:CAP]

    score_col = jnp.concatenate(score_cols, axis=0)
    spread = counted * (to_row(score_col) - score_col)
    small = jnp.exp(-jnp.abs(spread))
    softplus = jnp.maximum(spread, 0.0) + jnp.log1p(small)
    sigmoid = jnp.where(spread >= 0.0, 1.0, small) / (1.0 + small)
    both = jnp.abs(counted)
    pull_col = -weight_col * jnp.sum(counted * sigmoid, axis=1, keepdims=True)
    pair_col = weight_col * jnp.sum(both * softplus, axis=1, keepdims=True)
    pair_sum = 0.5 * jnp.sum(pair_col, axis=0, keepdims=True)
    pair_count = 0.5 * jnp.sum(
        jnp.sum(both, axis=1, keepdims=True), axis=0, keepdims=True
    )

    spread_rows[...] = jnp.where(lane_col == 0, score_col, pull_col)
    by_rank = [spread_rows[pl.ds(r, shards, stride=CAP), :] for r in range(CAP)]
    words = [x[:, 0:1] for x in by_rank] + [x[:, 1:2] for x in by_rank]
    words += [pair_sum, pair_count]
    message = jnp.zeros((shards, LANES), F32)
    for k, word in enumerate(words):
        message = jnp.where(lane_col == k, word, message)
    score_send[...] = message.reshape(shards, 1, LANES)

    def push_scores(i, carry):
        pltpu.make_async_remote_copy(
            score_send.at[i],
            score_recv.at[i],
            send_sem.at[2],
            recv_sem.at[2 * GROUPS],
            device_id={"shard": peer(shards - i)},
            device_id_type=MESH,
        ).start()
        return carry

    lax.fori_loop(1, shards, push_scores, 0)
    score_recv[0] = score_send[0]

    placed = [jnp.zeros((docs, LANES), F32) for _ in range(2)]
    for g in range(GROUPS):
        arrived(back, recv_sem.at[GROUPS + g], g)
        for k, part in enumerate(halves_of(back, g)):
            placed[k] = placed[k] + lax.dot_general(
                place[slots_of(g)],
                part,
                TN,
                preferred_element_type=F32,
            )
    for k in range(2):
        enc_ref[:, k * LANES : (k + 1) * LANES] = placed[k].astype(BF16)
    others = score_recv.at[pl.ds(1, shards - 1)]
    pltpu.make_async_copy(others, others, recv_sem.at[2 * GROUPS]).wait()
    message = score_recv[...].reshape(shards, LANES)
    sums = jnp.sum(message, axis=0, keepdims=True)
    pair_total = jnp.maximum(sums[:, 7:8], 1.0)
    found = lax.dot_general(
        message,
        named_f,
        TN,
        precision=lax.Precision.HIGHEST,
        preferred_element_type=F32,
    )
    score_out = jnp.zeros((1, docs), F32)
    grad_out = jnp.zeros((1, docs), F32)
    for r in range(CAP):
        score_out = score_out + jnp.where(rank == r, found[r : r + 1], 0.0)
        grad_out = grad_out + jnp.where(rank == r, found[CAP + r : CAP + r + 1], 0.0)
    small_ref[0:1, :] = score_out
    small_ref[1:2, :] = grad_out / pair_total
    small_ref[2:3, :] = jnp.broadcast_to(sums[:, 6:7] / pair_total, (1, docs))
    small_ref[3:8, :] = jnp.zeros((5, docs), F32)

    for at, ref in enumerate((send, back_send, score_send)):
        first = 1 if ref is score_send else CAP
        sent = ref.at[pl.ds(first, ref.shape[0] - first)]
        pltpu.make_async_copy(sent, sent, send_sem.at[at]).wait()


def body(
    features,
    owners,
    query_local,
    grades,
    query_weight,
    norm_gain,
    qkv_weight,
    out_weight,
    score_weight,
):
    shards = lax.axis_size("shard")
    heads = lax.axis_size("head")
    docs = features.shape[0]
    width, model = out_weight.shape
    slots = CAP * shards
    vmem = pl.BlockSpec(memory_space=pltpu.VMEM)
    hbm = pl.BlockSpec(memory_space=pltpu.HBM)
    dma = pltpu.SemaphoreType.DMA
    def row(x, at):
        return jnp.pad(
            x.reshape(1, -1), ((at, ROWS - 1 - at), (0, model - x.size))
        )

    integers = row(owners, 0) + row(query_local, 1) + row(grades, 2)
    floats = row(score_weight, 3) + row(norm_gain, 4) + row(query_weight, 5)
    small = integers.astype(F32) + floats
    blocks = pltpu.VMEM((slots, 2, LANES), BF16)
    words = pltpu.VMEM((shards, 1, LANES), F32)
    encoded, back_small = pl.pallas_call(
        functools.partial(layer_kernel, shards, heads, query_weight.shape[0]),
        out_shape=(
            jax.ShapeDtypeStruct((docs, width), BF16),
            jax.ShapeDtypeStruct((ROWS, docs), F32),
        ),
        in_specs=[hbm, vmem, hbm, hbm],
        out_specs=(vmem, vmem),
        scratch_shapes=[
            pltpu.VMEM((docs, width), BF16),
            pltpu.VMEM((3, model, width), BF16),
            pltpu.VMEM((heads, width, model), BF16),
            pltpu.VMEM((heads, ROWS, width), F32),
            blocks,
            blocks,
            words,
            words,
            pltpu.VMEM((slots, LANES), F32),
            pltpu.VMEM((heads, slots, width), BF16),
            pltpu.VMEM((slots, 3 * width), BF16),
            pltpu.VMEM((heads, slots, width), BF16),
            pltpu.VMEM((slots * max(SIXTEENTHS) // 16, model), F32),
            blocks,
            blocks,
            words,
            words,
            dma((3,)),
            dma((3,)),
            dma((2 * GROUPS + 1,)),
            dma((2 * GROUPS + 2, heads)),
            dma((2 * GROUPS + 2, heads)),
            dma((heads,)),
            dma((heads,)),
            dma,
            dma,
            dma((heads,)),
            dma((heads,)),
        ],
        compiler_params=pltpu.CompilerParams(
            collective_id=0, has_side_effects=True, vmem_limit_bytes=107 << 19
        ),
    )(
        features,
        small,
        jnp.transpose(qkv_weight, (1, 0, 2)),
        out_weight,
    )
    return encoded, back_small[0], back_small[1], back_small[2, 0]


def solution(mesh):
    placed = (
        P("shard", None),
        P("shard", None),
        P("shard"),
        P("shard"),
        P("shard"),
        P(),
        P(None, None, "head"),
        P("head", None),
        P("head"),
    )
    return jax.shard_map(
        body,
        mesh=mesh,
        in_specs=placed,
        out_specs=(P("shard", "head"), P("shard"), P("shard"), P()),
        check_vma=False,
    )
```

time: 79.9 us -> 73 us (0.914)
  local copies, waits for them, and re-layouts: 7.25 us -> 1.74 us
  Pallas kernels: 70.9 us -> 69.7 us
    unnamed x13 -> x1, local copies, waits for them, and re-layouts: 6.16 us -> 0.65 us
    pallas_call x1, Pallas kernels: 70.9 us -> 69.7 us  [body(): pl.pallas_call(functools.partial(layer_kernel, shards, heads, query_weigh...]
where the time goes in v4:
time: 73 us; the launch traced here: 72.8 us
  Pallas kernels  69.7 us (95%)
  local copies, waits for them, and re-layouts  1.74 us (2%)
  other arithmetic  0.77 us (1%)
    pallas_call x1, Pallas kernels, body(): pl.pallas_call(functools.partial(layer_kernel, shards, heads, query_weigh...  69.7 us

profile of v4, /device:TPU:1, one launch (start us, length us, event | category | flops | bytes accessed | tf_op | source)
XLA Modules:
  0.0 72.8 jit_solution(2670807482734454911)
XLA Ops:
  0.6 0.8 %add_add_fusion.inputs_ref = f32[8,1024]{1,0:T(8,128)S(1)} fusion(f32[1,16]{1,0:T(1,128)} %bitcast.18, f32[1,1024]{1,0:T(1,128)} %bitcast.11, f32[1,256]{1,0:T(1,128)} %bitcast.14, s32[1,256]{1,0:T(1,128)} %bitcast.15, s32[1,256]{1,0:T(1,128)} %bitcast.16, s32[1,256]{1,0:T(1,128)} %bitcast.17), kind=kLoop, calls=%fused_computation | loop fusion | flops 49152 | bytes 41024 | tf_op jit(solution)/shard_map/add | solution.py:493
  1.4 69.7 %shard_map.120 = (bf16[256,256]{1,0:T(8,128)(2,1)S(1)}, f32[8,256]{1,0:T(8,128)S(1)}) custom-call(bf16[256,1024]{1,0:T(8,128)(2,1)} %feat_hbm.1, f32[8,1024]{1,0:T(8,128)S(1)} %add_add_fusion.inputs_ref, bf16[3,1024,256]{2,1,0:T(8,128)(2,1)} %bitcast.10, bf16[256,1024]{1,0:T(8,128)(2,1)} %wout_hbm.1), custom_call_target="tpu_custom_call" | custom-call | tf_op jit(solution)/shard_map/pallas_call | solution.py:496
  71.1 0.6 fusion
  71.7 0.5 slice.11
  72.2 0.7 copy.14

commit v5 on v4

--- a/solution.py
+++ b/solution.py
@@ -322,26 +322,26 @@
         pair_copies.append(copy)
     project(GROUPS - 1, copies[GROUPS - 1])
 
+    keys_t = proj[:, width : 2 * width].T
     copies = []
     for g in range(GROUPS):
         for pair in range(width // LANES):
             at = pair * LANES
-            q2 = proj[slots_of(g), at : at + LANES]
-            k2 = proj[:, width + at : width + at + LANES]
+            q2 = proj[slots_of(g), at : at + LANES] * jnp.asarray(HEAD_DIM**-0.5, BF16)
+            k2 = keys_t[at : at + LANES, :]
             v2 = proj[:, 2 * width + at : 2 * width + at + LANES]
-            both_heads = None
-            for sub in range(LANES // HEAD_DIM):
-                mine = (lane_col // HEAD_DIM) == sub
-                q1 = jnp.where(mine, q2, jnp.zeros_like(q2))
-                scores = (
-                    lax.dot_general(q1, k2, NT, preferred_element_type=F32)
-                    * (HEAD_DIM**-0.5)
-                    + bias[slots_of(g), :]
-                )
-                expo = jnp.exp(scores - jnp.max(scores, axis=1, keepdims=True))
-                probs = (expo / jnp.sum(expo, axis=1, keepdims=True)).astype(BF16)
-                out = dot(probs, v2)
-                both_heads = out if sub == 0 else jnp.where(mine, out, both_heads)
+            halves = [
+                jnp.where((lane_col // HEAD_DIM) == sub, q2, jnp.zeros_like(q2))
+                for sub in range(LANES // HEAD_DIM)
+            ]
+            scores = dot(jnp.concatenate(halves, axis=0), k2) + jnp.concatenate(
+                [bias[slots_of(g), :]] * 2, axis=0
+            )
+            expo = jnp.exp(scores - jnp.max(scores, axis=1, keepdims=True))
+            whole = 1.0 / jnp.sum(expo, axis=1, keepdims=True)
+            out = dot(expo.astype(BF16), v2) * whole
+            rows = (cut[g + 1] - cut[g]) * CAP
+            both_heads = jnp.where(lane_col < HEAD_DIM, out[:rows], out[rows:])
             context[head, slots_of(g), at : at + LANES] = both_heads.astype(BF16)
         own = context.at[head, slots_of(g)]
         copies.append(exchange(own, own, GROUPS + g))

time: 73 us -> 70.5 us (0.966)
  Pallas kernels: 69.7 us -> 67.2 us
    pallas_call x1, Pallas kernels: 69.7 us -> 67.2 us  [body(): pl.pallas_call(functools.partial(layer_kernel, shards, heads, query_weigh...]
where the time goes in v5:
time: 70.5 us; the launch traced here: 70.4 us
  Pallas kernels  67.2 us (95%)
  local copies, waits for them, and re-layouts  1.74 us (2%)
  other arithmetic  0.77 us (1%)
    pallas_call x1, Pallas kernels, body(): pl.pallas_call(functools.partial(layer_kernel, shards, heads, query_weigh...  67.2 us

profile of v5, /device:TPU:1, one launch (start us, length us, event | category | flops | bytes accessed | tf_op | source)
XLA Modules:
  0.0 70.4 jit_solution(16091050493173794478)
XLA Ops:
  0.6 0.8 %add_add_fusion.inputs_ref = f32[8,1024]{1,0:T(8,128)S(1)} fusion(f32[1,16]{1,0:T(1,128)} %bitcast.18, f32[1,1024]{1,0:T(1,128)} %bitcast.11, f32[1,256]{1,0:T(1,128)} %bitcast.14, s32[1,256]{1,0:T(1,128)} %bitcast.15, s32[1,256]{1,0:T(1,128)} %bitcast.16, s32[1,256]{1,0:T(1,128)} %bitcast.17), kind=kLoop, calls=%fused_computation | loop fusion | flops 49152 | bytes 41024 | tf_op jit(solution)/shard_map/add | solution.py:493
  1.4 67.2 %shard_map.120 = (bf16[256,256]{1,0:T(8,128)(2,1)S(1)}, f32[8,256]{1,0:T(8,128)S(1)}) custom-call(bf16[256,1024]{1,0:T(8,128)(2,1)} %feat_hbm.1, f32[8,1024]{1,0:T(8,128)S(1)} %add_add_fusion.inputs_ref, bf16[3,1024,256]{2,1,0:T(8,128)(2,1)} %bitcast.10, bf16[256,1024]{1,0:T(8,128)(2,1)} %wout_hbm.1), custom_call_target="tpu_custom_call" | custom-call | tf_op jit(solution)/shard_map/pallas_call | solution.py:496
  68.6 0.6 fusion
  69.2 0.5 slice.11
  69.7 0.7 copy.14

commit v6 on v5

--- a/solution.py
+++ b/solution.py
@@ -11,7 +11,7 @@
 HEAD_DIM = 64
 CAP = 3
 ROWS = 8
-SIXTEENTHS = (4, 4, 4, 2, 2)
+SIXTEENTHS = (2, 4, 4, 4, 2)
 GROUPS = len(SIXTEENTHS)
 LANES = 128
 eps_norm = 1e-06
@@ -383,9 +383,8 @@
             ).start()
             return carry
 
-        lax.fori_loop(
-            max(1, cut[g]), cut[g + 1], push_back, 0, unroll=g == GROUPS - 1
-        )
+        if g < GROUPS - 1:
+            lax.fori_loop(max(1, cut[g]), cut[g + 1], push_back, 0)
     back[0:CAP] = back_send[0:CAP]
 
     score_col = jnp.concatenate(score_cols, axis=0)
@@ -422,6 +421,7 @@
         return carry
 
     lax.fori_loop(1, shards, push_scores, 0)
+    lax.fori_loop(cut[GROUPS - 1], shards, push_back, 0)
     score_recv[0] = score_send[0]
 
     placed = [jnp.zeros((docs, LANES), F32) for _ in range(2)]

time: 70.5 us -> 70.7 us (level)
  no operation moved by 1% of the time
where the time goes in v6:
time: 70.7 us; the launch traced here: 70.6 us
  Pallas kernels  67.4 us (95%)
  local copies, waits for them, and re-layouts  1.74 us (2%)
  other arithmetic  0.77 us (1%)
    pallas_call x1, Pallas kernels, body(): pl.pallas_call(functools.partial(layer_kernel, shards, heads, query_weigh...  67.4 us

profile of v6, /device:TPU:1, one launch (start us, length us, event | category | flops | bytes accessed | tf_op | source)
XLA Modules:
  0.0 70.6 jit_solution(1833118644548275773)
XLA Ops:
  0.6 0.8 %add_add_fusion.inputs_ref = f32[8,1024]{1,0:T(8,128)S(1)} fusion(f32[1,16]{1,0:T(1,128)} %bitcast.18, f32[1,1024]{1,0:T(1,128)} %bitcast.11, f32[1,256]{1,0:T(1,128)} %bitcast.14, s32[1,256]{1,0:T(1,128)} %bitcast.15, s32[1,256]{1,0:T(1,128)} %bitcast.16, s32[1,256]{1,0:T(1,128)} %bitcast.17), kind=kLoop, calls=%fused_computation | loop fusion | flops 49152 | bytes 41024 | tf_op jit(solution)/shard_map/add | solution.py:493
  1.4 67.4 %shard_map.120 = (bf16[256,256]{1,0:T(8,128)(2,1)S(1)}, f32[8,256]{1,0:T(8,128)S(1)}) custom-call(bf16[256,1024]{1,0:T(8,128)(2,1)} %feat_hbm.1, f32[8,1024]{1,0:T(8,128)S(1)} %add_add_fusion.inputs_ref, bf16[3,1024,256]{2,1,0:T(8,128)(2,1)} %bitcast.10, bf16[256,1024]{1,0:T(8,128)(2,1)} %wout_hbm.1), custom_call_target="tpu_custom_call" | custom-call | tf_op jit(solution)/shard_map/pallas_call | solution.py:496
  68.9 0.6 fusion
  69.4 0.5 slice.11
  69.9 0.7 copy.14
